TPU v7x, 256 devices: a whole 4x4x8 slice. The times are simulated.
256 devices in a mesh: samp: 16 (over z, core), var: 16 (over x, y).
Axes of the slice: x: 4, y: 4, z: 8, core: 2. Of those that a mesh axis runs over, the one named last changes fastest.
Arguments:
- geno: bfloat16 [8192, 32768], P('samp', 'var'), may hold values from 0 to 2
- covar: bfloat16 [8192, 32], P('samp')
- pheno: float32 [8192, 64], P('samp', 'var')
- perm: int32 [48, 8192], P(None, 'samp'), may hold values from 0 to 8191, each once within a row
- windows: int32 [64, 2], replicated, may hold values from 0 to 32768, as said below
Outputs:
- curves: float32 [64, 64], P('var')
- peak: float32 [64, 48], P('var')
Inputs may be any that keep to these rules, and one draw needn't show every extreme that they name: Each gene g has windows[g, 0] < windows[g, 1], and its window lies within variants g // 4 * 2048 - 1024 to (g // 4 + 1) * 2048 + 1024, cut to the genome; in each band the first gene's window begins and the last gene's window ends at those bounds (cut to the genome).
All inputs are finite; a program needn't handle non-finite values.
Results may differ from a plain program's by a relative error of at most 0.0016.
Values may be sent and summed in bfloat16 or wider, within the bound.
A program may use at most 64 MiB of HBM per device.

v0:
```python
import jax
import jax.numpy as jnp
from jax import lax
from jax.sharding import PartitionSpec as P

LEVELS = 64


EPS = 1e-06
LEVMAX = 40.0


def padded(block, sides, width):
    for axis, dim in sides:
        count = lax.axis_size(axis)
        forward = [(i, i + 1) for i in range(count - 1)]
        backward = [(target, source) for source, target in forward]
        low = lax.ppermute(
            lax.slice_in_dim(block, block.shape[dim] - width, None, axis=dim), axis, forward
        )
        high = lax.ppermute(lax.slice_in_dim(block, 0, width, axis=dim), axis, backward)
        block = jnp.concatenate([low, block, high], axis=dim)
    return block


def factor_solve(factor, rhs):
    lower_part = lax.linalg.triangular_solve(factor, rhs, left_side=True, lower=True)
    return lax.linalg.triangular_solve(
        factor, lower_part, left_side=True, lower=True, transpose_a=True
    )


def per_device(geno, covar, pheno, perm, windows):
    nrow = geno.shape[0]
    vband = geno.shape[1]
    gband = pheno.shape[1]
    nperm = perm.shape[0]
    nshard = lax.axis_size("samp")
    band = lax.axis_index("var")
    shard = lax.axis_index("samp")
    ones = jnp.ones((nrow, 1), jnp.bfloat16)
    xlow = jnp.concatenate([ones, covar], axis=1)
    xmat = xlow.astype(jnp.float32)
    anchor = band * vband
    cross_part = jnp.dot(xmat.T, xmat, precision=lax.Precision.HIGHEST)
    ycross_part = jnp.dot(xmat.T, pheno, precision=lax.Precision.HIGHEST)
    gcross_part = jnp.dot(xlow.T, geno, preferred_element_type=jnp.float32)
    cross, ycross, gcross = lax.psum((cross_part, ycross_part, gcross_part), "samp")
    factor = jnp.linalg.cholesky(cross)
    beta_y = factor_solve(factor, ycross)
    beta_g = factor_solve(factor, gcross)
    yres = pheno - jnp.dot(xmat, beta_y, precision=lax.Precision.HIGHEST)
    gres = geno.astype(jnp.float32) - jnp.dot(xmat, beta_g, precision=lax.Precision.HIGHEST)
    gsq, ysq = lax.psum((jnp.sum(gres * gres, axis=0), jnp.sum(yres * yres, axis=0)), "samp")
    ynorm = jnp.sqrt(ysq + EPS)
    yall = lax.all_gather(yres, "samp", axis=0, tiled=True)
    shuffled = jnp.take(yall, perm, axis=0)
    scaled = (shuffled / ynorm[None, None, :]).astype(jnp.bfloat16)
    ypb = jnp.transpose(scaled, (1, 2, 0)).reshape(nrow, gband * nperm)
    ycols = padded(ypb, (("var", 1),), gband * nperm)
    first = band * gband - gband
    ngroup = 3 * gband
    proj = jnp.dot(xlow.T, ycols, preferred_element_type=jnp.float32)
    rows = geno.shape[1] // nshard
    direct = lax.dot_general(
        geno, ycols, (((0,), (0,)), ((), ())), preferred_element_type=jnp.float32
    )
    adjust = lax.dot_general(
        beta_g, proj, (((0,), (0,)), ((), ())), precision=lax.Precision.HIGHEST
    )
    partial_sums = lax.psum_scatter(direct - adjust, "samp", scatter_dimension=0, tiled=True)
    local_start = shard * rows
    blank = jnp.zeros((gband, 2), jnp.int32)
    padded_win = jnp.concatenate([blank, windows, blank], axis=0)
    local_sq = lax.dynamic_slice_in_dim(gsq, local_start, rows, 0)
    corr = partial_sums / jnp.sqrt(local_sq + EPS)[:, None]
    squared = (corr * corr).reshape(rows, ngroup, nperm)
    window = lax.dynamic_slice_in_dim(padded_win, first + gband, ngroup, 0)
    position = anchor + local_start + jnp.arange(rows, dtype=jnp.int32)
    inside = (position[:, None] >= window[None, :, 0]) & (position[:, None] < window[None, :, 1])
    part_max = jnp.max(jnp.where(inside[:, :, None], squared, 0.0), axis=0)
    merged = lax.pmax(part_max, "samp")
    trio = merged.reshape(3, gband, nperm)
    beside_all = padded(trio, (("var", 0),), 1)
    peak_sq = jnp.maximum(jnp.maximum(beside_all[0], beside_all[2]), beside_all[4])
    peak = jnp.float32(nrow * nshard) * peak_sq
    levels = LEVMAX * jnp.arange(LEVELS, dtype=jnp.float32) / (LEVELS - 1)
    curves = jnp.mean(jax.nn.sigmoid(peak[:, :, None] - levels[None, None, :]), axis=1)
    return (curves, peak)


def solution(mesh):
    in_specs = (P("samp", "var"), P("samp", None), P("samp", "var"), P(None, "samp"), P())
    out_specs = (P("var", None), P("var", None))
    return jax.shard_map(
        per_device, mesh=mesh, in_specs=in_specs, out_specs=out_specs, check_vma=False
    )
```

profile of v0, /device:TPU:1, one launch (start us, length us, event | category | flops | bytes accessed | tf_op | source)
XLA Modules:
  0.0 331.5 jit_solution(14357562704021606660)
XLA Ops:
  7.2 0.0 all-reduce.5.cloned.1.call-start
  7.2 2.8 fusion.7
  10.0 0.0 all-reduce.5.cloned.1.call-update
  10.1 0.0 reduce-scatter.2.cloned.1.call-start
  10.1 0.1 fusion.12
  10.3 0.1 fusion.10
  10.4 48.8 %all-reduce.2 = (f32[33,33]{0,1:T(8,128)S(1)}, f32[33,4]{0,1:T(4,128)S(1)}) all-reduce(f32[33,33]{0,1:T(8,128)S(1)} %fusion.12, f32[33,4]{0,1:T(4,128)S(1)} %fusion.10), channel_id=1, replica_groups=mesh['samp'=16,'var'=16] {'samp'}, use_global_device_ids=true, to_apply=%region_0.0 | all-reduce | flops 1221 | bytes 9768 | tf_op jit(solution)/shard_map/psum | solution.py:48
  59.2 0.1 copy.15
  59.3 3.0 cholesky.16
  62.4 0.6 compare_reduce_fusion
  63.0 0.7 fusion.14
  63.7 2.5 custom-call.12
  66.2 0.2 fusion.21
  66.4 0.1 fusion.19
  66.5 0.3 multiply_reduce_fusion.1
  66.8 17.9 %all_gather.3 = f32[8192,4]{0,1:T(4,128)S(1)} all-gather(f32[512,4]{0,1:T(4,128)S(1)} %get-tuple-element.11), channel_id=1, replica_groups=mesh['samp'=16,'var'=16] {'samp'}, dimensions={0}, use_global_device_ids=true | all-gather | bytes 139264 | tf_op jit(solution)/shard_map/all_gather | solution.py:56
  84.7 2.7 copy.16
  87.4 83.5 %gather_fusion = f32[24576,4]{1,0:T(8,128)} fusion(f32[8192,4]{1,0:T(8,128)} %copy.16, s32[24576]{0:T(1024)S(1)} %broadcast_clamp_fusion), kind=kCustom, calls=%fused_computation | custom fusion | bytes 884736 | tf_op jit(solution)/shard_map/jit(_take)/gather | solution.py:57
  170.9 7.8 %copy.17 = f32[48,512,4]{1,0,2:T(8,128)S(1)} copy(f32[48,512,4]{2,1,0:T(8,128)} %bitcast.54) | data formatting | bytes 786432 | tf_op jit(solution)/shard_map/jit(_take)/gather | solution.py:57
  178.7 0.0 all-reduce.5.cloned.1.call-done
  178.7 1.4 fusion.17
  180.2 0.4 fusion.15
  180.6 2.2 multiply_reduce_fusion
  182.8 23.9 %all-reduce.1 = (f32[4]{0:T(128)S(1)}, f32[2048]{0:T(1024)S(1)}) all-reduce(f32[4]{0:T(128)S(1)} %get-tuple-element.10, f32[2048]{0:T(1024)S(1)} %multiply_reduce_fusion), channel_id=1, replica_groups=mesh['samp'=16,'var'=16] {'samp'}, use_global_device_ids=true, to_apply=%region_5.6 | all-reduce | flops 2052 | bytes 16416 | tf_op jit(solution)/shard_map/psum | solution.py:54
  206.8 0.1 fusion.1
  206.9 3.2 collective-permute-start
  210.1 1.3 collective-permute-start.1
  211.4 1.3 collective-permute-done
  212.7 3.8 %collective-permute-done.1 = bf16[512,192]{0,1:T(8,128)(2,1)S(1)} collective-permute-done((bf16[512,192]{0,1:T(8,128)(2,1)S(1)}, bf16[512,192]{0,1:T(8,128)(2,1)S(1)}, u32[]{:S(2)}, u32[]{:S(2)}) %collective-permute-start.1) | collective-permute-done | bytes 196640 | tf_op jit(solution)/shard_map/ppermute | solution.py:21
  216.5 0.3 fusion.2
  216.8 4.0 %fusion.34 = f32[2048,576]{0,1:T(8,128)S(1)} fusion(f32[33,2048]{1,0:T(8,128)S(1)} %fusion.15, f32[33,576]{1,0:T(8,128)S(1)} %fusion.2), kind=kOutput, calls=%fused_computation.65 | convolution fusion | flops 467140608 | bytes 5064960 | tf_op jit(solution)/shard_map/dot_general | solution.py:68
  220.8 3.6 %bitcast_subtract_fusion = f32[2048,576]{0,1:T(8,128)} fusion(f32[2048,576]{0,1:T(8,128)S(1)} %fusion.34, bf16[512,2048]{1,0:T(8,128)(2,1)S(1)} %copy-done, bf16[512,192]{0,1:T(8,128)(2,1)S(1)} %collective-permute-done.1, bf16[512,192]{0,1:T(8,128)(2,1)S(1)} %bitcast.58, bf16[512,192]{0,1:T(8,128)(2,1)S(1)} %collective-permute-done), kind=kOutput, calls=%fused_computation.1 | convolution fusion | flops 1210908672 | bytes 12124160 | tf_op jit(solution)/shard_map/dot_general | solution.py:65
  224.4 0.0 reduce-scatter.2.cloned.1.call-update
  224.4 0.6 copy-done.5
  225.0 0.1 pad_add_fusion
  225.1 0.1 constant_dynamic-slice_fusion
  225.2 0.1 compare_and_fusion
  225.3 0.1 add_sqrt_fusion
  225.4 62.5 %reduce-scatter.2.cloned.1.call-done = f32[128,576]{0,1:T(8,128)} async-done(((f32[2048,576]{0,1:T(8,128)}), f32[128,576]{0,1:T(8,128)}) %reduce-scatter.2.cloned.1.call-update) | async-done | bytes 294928 | tf_op jit(solution)/shard_map/reduce_scatter | solution.py:71
  287.9 1.1 select_reduce_fusion
  289.1 0.1 reduce_max.12
  289.1 27.2 %pmax.7 = f32[12,48]{1,0:T(8,128)S(1)} all-reduce(f32[12,48]{1,0:T(8,128)S(1)} %reduce_max.12), channel_id=1, replica_groups=mesh['samp'=16,'var'=16] {'samp'}, use_global_device_ids=true, to_apply=%region_11.12 | all-reduce | flops 576 | bytes 4608 | tf_op jit(solution)/shard_map/pmax | solution.py:82
  316.3 3.3 collective-permute-start.2
  319.6 1.3 collective-permute-start.3
  320.9 0.0 collective-permute-done.2
  320.9 3.0 collective-permute-done.3
  324.0 0.1 fusion.3
  324.1 0.6 broadcast_multiply_fusion
  (25 shorter events, 0.2 us)
Async XLA Ops:
  7.2 3.0 copy-start.1
  7.2 3.1 copy-start.3
  7.2 171.5 %all-reduce.5.cloned.1.call-start = ((), (), s32[]{:S(2)}) async-start(), calls=%async_computation.1 | async-start | bytes 655360 | tf_op jit(solution)/shard_map/psum | solution.py:48
  10.1 277.8 %reduce-scatter.2.cloned.1.call-start = ((), (), s32[]{:S(2)}) async-start(), calls=%async_computation.2 | async-start | bytes 5013504 | tf_op jit(solution)/shard_map/reduce_scatter | solution.py:71
  84.7 2.7 copy-start.2
  170.9 9.7 %copy-start = (bf16[512,2048]{1,0:T(8,128)(2,1)S(1)}, bf16[512,2048]{1,0:T(8,128)(2,1)}, u32[]{:S(2)}) copy-start(bf16[512,2048]{1,0:T(8,128)(2,1)} %param.5) | copy-start | bytes 6291460
  206.9 5.8 %collective-permute-start = (bf16[512,192]{0,1:T(8,128)(2,1)S(1)}, bf16[512,192]{0,1:T(8,128)(2,1)S(1)}, u32[]{:S(2)}, u32[]{:S(2)}) collective-permute-start(bf16[512,192]{0,1:T(8,128)(2,1)S(1)} %bitcast.55), channel_id=1, source_target_pairs={{0,1},{1,2},{2,3},{3,4},{4,5},{5,6},{6,7},{7,8},{8,9},{9,10},{10,1... | collective-permute-start | bytes 589832 | tf_op jit(solution)/shard_map/ppermute | solution.py:18
  210.1 6.4 %collective-permute-start.1 = (bf16[512,192]{0,1:T(8,128)(2,1)S(1)}, bf16[512,192]{0,1:T(8,128)(2,1)S(1)}, u32[]{:S(2)}, u32[]{:S(2)}) collective-permute-start(bf16[512,192]{0,1:T(8,128)(2,1)S(1)} %bitcast.56), channel_id=1, source_target_pairs={{1,0},{2,1},{3,2},{4,3},{5,4},{6,5},{7,6},{8,7},{9,8},{10,9},{11,1... | collective-permute-start | bytes 589832 | tf_op jit(solution)/shard_map/ppermute | solution.py:21
  224.4 0.7 copy-start.5
  316.3 4.6 %collective-permute-start.2 = (f32[1,4,48]{2,1,0:T(4,128)S(1)}, f32[1,4,48]{2,1,0:T(4,128)S(1)}, u32[]{:S(2)}, u32[]{:S(2)}) collective-permute-start(f32[1,4,48]{2,1,0:T(4,128)S(1)} %get-tuple-element.6), channel_id=1, source_target_pairs={{0,1},{1,2},{2,3},{3,4},{4,5},{5,6},{6,7},{7,8},{8,9},{9,10},{10,1... | collective-permute-start | bytes 2312 | tf_op jit(solution)/shard_map/ppermute | solution.py:18
  319.6 4.3 %collective-permute-start.3 = (f32[1,4,48]{2,1,0:T(4,128)S(1)}, f32[1,4,48]{2,1,0:T(4,128)S(1)}, u32[]{:S(2)}, u32[]{:S(2)}) collective-permute-start(f32[1,4,48]{2,1,0:T(4,128)S(1)} %get-tuple-element.7), channel_id=1, source_target_pairs={{1,0},{2,1},{3,2},{4,3},{5,4},{6,5},{7,6},{8,7},{9,8},{10,9},{11,1... | collective-permute-start | bytes 2312 | tf_op jit(solution)/shard_map/ppermute | solution.py:21
  324.0 0.7 copy-start.4
Sparse Core Ops, SparseCore 0:
  10.3 111.1 all-reduce.4
  224.5 63.3 reduce-scatter.1
where the time goes:
time: 334 us; the launch traced here: 332 us
  blocking collectives  118 us (35%)
  local copies, waits for them, and re-layouts  94.8 us (28%)
  waiting for transfers between devices  70.7 us (21%)
  matrix products  15.5 us (5%)
  between operations  14.3 us (4%)
  starting transfers between devices  9.13 us (3%)
  other arithmetic  9.13 us (3%)
    gather x2, local copies, waits for them, and re-layouts, per_device(): shuffled = jnp.take(yall, perm, axis=0)  91.3 us
    reduce_scatter x1, waiting for transfers between devices, per_device(): lax.psum_scatter(direct - adjust, 'samp', scatter_dimension=0, tiled=True)  62.5 us
    psum x1, blocking collectives, per_device(): lax.psum((cross_part, ycross_part, gcross_part), 'samp')  48.8 us
    pmax x1, blocking collectives, per_device(): merged = lax.pmax(part_max, 'samp')  27.2 us
    psum x1, blocking collectives, per_device(): lax.psum((jnp.sum(gres * gres, axis=0), jnp.sum(yres * yres, axis=0)), 's...  23.9 us
    all_gather x1, blocking collectives, per_device(): yall = lax.all_gather(yres, 'samp', axis=0, tiled=True)  17.9 us
    ppermute x2, waiting for transfers between devices, padded(): lax.ppermute(lax.slice_in_dim(block, 0, width, axis=dim), axis, backward)  6.83 us
  transfers between devices with their start and end apart: 6, of which 4 were waited for; matrix products, arithmetic and copies ran while one was open for 31% of the time, Pallas kernels for 0%

commit v1 on v0

v1 whole, which is shorter than its diff:
```python
import functools

import jax
import jax.numpy as jnp
from jax import lax
from jax.experimental import pallas as pl
from jax.experimental.pallas import tpu as pltpu
from jax.sharding import PartitionSpec as P

MESH = pl.DeviceIdType.MESH
F32 = jnp.float32
BF16 = jnp.bfloat16
HIGH = lax.Precision.HIGHEST

EPS = 1e-06
LEVMAX = 40.0
LEVELS = 64

NZ = 8
NB = 16
NS = 512
NSAMP = 8192
VB = 2048
VH = 1024
NG = 4
NP = 48
NC = 32
XR = 48
ONE = 44
SPARE = 45
ROWS = NG * NP
CH = ROWS // NZ
DW = VH + 128
HOPS = (4, 3)


def nt(a, b):
    return lax.dot_general(a, b, (((1,), (1,)), ((), ())), preferred_element_type=F32)


def mm(a, b, precision=None):
    return lax.dot_general(
        a, b, (((1,), (0,)), ((), ())), preferred_element_type=F32, precision=precision
    )


def kernel(
    upto,
    geno, covt, phet, perm, win,
    cur_ref, peak_ref,
    xa, p8, gs, gcp, gr, ga, gm, yt, yo, yn, ds, rb, xs, xm, fm,
    loc_sem, xg_s, xg_r, ring_s, ring_r, fw_s, fw_r, gr_s, gr_r, ga_s, ga_r,
    y_s, y_r, rs_s, rs_r, x_s, x_r, f_s, f_r,
):
    s = lax.axis_index("samp")
    b = lax.axis_index("var")
    z = lax.div(s, 2)
    c = lax.rem(s, 2)
    oc = 1 - c
    up_band = lax.rem(b + 1, NB)
    down_band = lax.rem(b + NB - 1, NB)
    nbr = lax.rem(b + 2 * c - 1 + NB, NB)

    def zc(k):
        return lax.rem(z + (k + NZ), NZ)

    def dev(zz, cc, bb):
        return {"samp": zz * 2 + cc, "var": bb}

    def copy(src, dst, ss, rs, to):
        return pltpu.make_async_remote_copy(
            src_ref=src, dst_ref=dst, send_sem=ss, recv_sem=rs,
            device_id=to, device_id_type=MESH,
        )

    pend = []

    def start(src, dst, ss, rs, to):
        d = copy(src, dst, ss, rs, to)
        d.start()
        pend.append(d)

    def landed(dst, rs):
        copy(dst, dst, rs, rs, dev(z, oc, b)).wait_recv()

    def finish():
        for d in pend:
            d.wait_send()

    def stop():
        finish()
        cur_ref[...] = jnp.zeros_like(cur_ref)
        peak_ref[...] = jnp.zeros_like(peak_ref)

    own_geno = pltpu.make_async_copy(
        geno.at[:, pl.ds(pl.multiple_of(c * VH, VH), VH)], gs.at[c], loc_sem
    )
    own_geno.start()
    p8[0:4, :] = phet[...]
    p8[4:8, :] = phet[...]
    full = p8[...]
    hi = full.astype(BF16).astype(F32)
    rest = full - hi
    mid = rest.astype(BF16).astype(F32)
    low = (rest - mid).astype(BF16).astype(F32)
    row8 = lax.broadcasted_iota(jnp.int32, (8, NS), 0)
    block_a = jnp.where(row8 < 4, hi, mid)
    block_b = jnp.where(row8 < 4, low, jnp.where(row8 == 4, 1.0, 0.0))
    xa[s] = jnp.concatenate([covt[...].astype(F32), block_a, block_b], axis=0).astype(BF16)

    barrier = pltpu.get_barrier_semaphore()
    peers = [dev(zc(k), c, b) for k in range(1, NZ)] + [dev(z, oc, b)]
    peers += [dev(z, cc, bb) for cc in (0, 1) for bb in (up_band, down_band)]
    for peer in peers:
        pl.semaphore_signal(barrier, inc=1, device_id=peer, device_id_type=MESH)
    pl.semaphore_wait(barrier, len(peers))

    start(
        geno.at[:, pl.ds(pl.multiple_of(oc * VH, VH), VH)], gs.at[c], xg_s, xg_r, dev(z, oc, b)
    )

    def slot(k, cc):
        return zc(k) * 2 + cc

    def send_right(t):
        q = slot(-t, c)
        start(xa.at[q], xa.at[q], ring_s.at[0, t], ring_r.at[0, t], dev(zc(1), c, b))

    def send_left(t):
        q = slot(t, c)
        start(xa.at[q], xa.at[q], ring_s.at[1, t], ring_r.at[1, t], dev(zc(-1), c, b))

    def hand_over(k):
        q = slot(k, c)
        start(xa.at[q], xa.at[q], fw_s.at[k + 4], fw_r.at[k + 4], dev(z, oc, b))

    def got_right(t):
        landed(xa.at[slot(-1 - t, c)], ring_r.at[0, t])

    def got_left(t):
        landed(xa.at[slot(1 + t, c)], ring_r.at[1, t])

    send_right(0)
    send_left(0)
    hand_over(0)
    got_right(0)
    send_right(1)
    hand_over(-1)
    got_left(0)
    send_left(1)
    hand_over(1)

    own_geno.wait()
    landed(gs.at[oc], xg_r)
    landed(xa.at[slot(0, oc)], fw_r.at[4])
    gpart = mm(xa[z * 2], gs[0]) + mm(xa[z * 2 + 1], gs[1])

    got_right(1)
    send_right(2)
    hand_over(-2)
    got_left(1)
    send_left(2)
    hand_over(2)

    mean = gpart[ONE:ONE + 1, :] * (1.0 / (2 * NS))

    def spread(i, acc):
        blk = gs[lax.div(i, 32), pl.ds(pl.multiple_of(lax.rem(i, 32) * 16, 16), 16), :].astype(F32)
        dif = blk - mean
        return acc + dif * dif

    acc = lax.fori_loop(0, 64, spread, jnp.zeros((16, VH), F32))
    local_sq = jnp.sum(acc, axis=0, keepdims=True)
    rowg = lax.broadcasted_iota(jnp.int32, (XR, VH), 0)
    gpart = jnp.where(rowg == SPARE, local_sq, gpart)
    for j in range(NZ):
        gcp[j] = gpart[:, j * 128:(j + 1) * 128]
    for k in range(1, NZ):
        start(gcp.at[zc(k)], gr.at[z], gr_s.at[k], gr_r.at[NZ - k], dev(zc(k), c, b))

    got_right(2)
    send_right(3)
    hand_over(-3)
    got_left(2)
    hand_over(3)
    got_right(3)
    hand_over(-4)
    for k in (-1, 1, -2, 2, -3, 3, -4):
        landed(xa.at[slot(k, oc)], fw_r.at[k + 4])
    if upto == 1:
        for k in range(1, NZ):
            landed(gr.at[zc(k)], gr_r.at[k])
        stop()
        return

    def gram_step(i, acc):
        blk = xa[i]
        return acc + nt(blk, blk)

    gram = lax.fori_loop(0, 2 * NZ, gram_step, jnp.zeros((XR, XR), F32))
    gm[...] = jnp.zeros_like(gm)
    gm[:, 0:XR] = gram
    a = gm[...]
    colmean = a[:, ONE:ONE + 1] * (1.0 / NSAMP)
    row = lax.broadcasted_iota(jnp.int32, (XR, 128), 0)
    lane = lax.broadcasted_iota(jnp.int32, (XR, 128), 1)
    for k in (ONE,) + tuple(range(NC)):
        q = a[:, k:k + 1]
        r = a[k:k + 1, :]
        inv = 1.0 / a[k:k + 1, k:k + 1]
        rr = r * inv
        nxt = a - q * rr
        nxt = jnp.where(row == k, rr, nxt)
        nxt = jnp.where(lane == k, jnp.where(row == k, -inv, q * inv), nxt)
        a = nxt
    in_row = (row < NC) | (row == ONE)
    in_lane = (lane < NC) | (lane == ONE)
    gm[...] = jnp.where(in_row & in_lane, -a, 0.0)

    for k in range(1, NZ):
        landed(gr.at[zc(k)], gr_r.at[k])
    gr[z] = gcp[z]
    tot = gr[0]
    for j in range(1, NZ):
        tot = tot + gr[j]
    mu = tot[ONE:ONE + 1, :] * (1.0 / NSAMP)
    between = jnp.zeros((1, 128), F32)
    for j in range(NZ):
        off = gr[j, ONE:ONE + 1, :] * (1.0 / (2 * NS)) - mu
        between = between + off * off
    ga[z] = tot + jnp.where(row == SPARE, between * (2.0 * NS), 0.0)
    for k in range(1, NZ):
        start(ga.at[z], ga.at[z], ga_s.at[k], ga_r.at[NZ - k], dev(zc(k), c, b))

    ba = a[32:40, :]
    beta = ba + pltpu.roll(ba, 4, axis=0) + a[40:48, :]
    r8 = lax.broadcasted_iota(jnp.int32, (8, 128), 0)
    l8 = lax.broadcasted_iota(jnp.int32, (8, 128), 1)
    pick = (l8 == r8 + 32) | (l8 == r8 + 36) | (l8 == r8 + 40)
    coef = jnp.where(pick & (r8 < 4), 1.0, 0.0)
    coef = jnp.where(((l8 < NC) | (l8 == ONE)) & (r8 < 4), -beta, coef)
    c_hi = coef.astype(BF16).astype(F32)
    c_rest = coef - c_hi
    c_mid = c_rest.astype(BF16).astype(F32)
    c_low = c_rest - c_mid
    coefs = jnp.concatenate([c_hi, c_mid, c_low], axis=0)[:, 0:XR].astype(BF16)

    def resid(i, acc):
        t = mm(coefs, xa[i])
        y = (t[16:24] + t[8:16]) + t[0:8]
        yt[i] = y
        return acc + y * y

    ysq = jnp.sum(
        lax.fori_loop(0, 2 * NZ, resid, jnp.zeros((8, NS), F32)), axis=1, keepdims=True
    )
    ynorm = jnp.sqrt(ysq + EPS)

    def scale(i, carry):
        yt[i] = (yt[i] / ynorm).astype(BF16).astype(F32)
        return carry

    lax.fori_loop(0, 2 * NZ, scale, 0)
    if upto == 2:
        for k in range(1, NZ):
            landed(ga.at[zc(k)], ga_r.at[k])
        stop()
        return

    for blk in range(NS // 128):
        idx = perm[:, blk * 128:(blk + 1) * 128]
        ilo = lax.bitwise_and(idx, 127)
        ihi = lax.shift_right_logical(idx, 7)

        def look(i, accs, ilo=ilo, ihi=ihi):
            accs = list(accs)
            for q in range(4):
                hit = ihi == i * 4 + q
                for g in range(NG):
                    src = jnp.broadcast_to(yt[i, g:g + 1, q * 128:(q + 1) * 128], (NP, 128))
                    got = jnp.take_along_axis(src, ilo, axis=1, mode="promise_in_bounds")
                    accs[g] = jnp.where(hit, got, accs[g])
            return tuple(accs)

        accs = lax.fori_loop(
            0, 2 * NZ, look, tuple(jnp.zeros((NP, 128), F32) for _ in range(NG))
        )
        for g in range(NG):
            yo[c, g * NP:(g + 1) * NP, blk * 128:(blk + 1) * 128] = accs[g].astype(BF16)
    if upto == 3:
        for k in range(1, NZ):
            landed(ga.at[zc(k)], ga_r.at[k])
        stop()
        return

    start(yo.at[c], yo.at[c], y_s.at[0], y_r.at[0], dev(z, oc, b))
    start(yo.at[c], yn.at[c], y_s.at[1], y_r.at[1 + c], dev(z, 0, up_band))
    start(yo.at[c], yn.at[c], y_s.at[2], y_r.at[1 + c], dev(z, 1, down_band))

    def product(y, kind):
        ds[kind, :, 0:VH] = mm(y[0], gs[0]) + mm(y[1], gs[1])
        ds[kind, :, VH:DW] = jnp.zeros((ROWS, 128), F32)
        ds[kind, :, VH:VH + XR] = nt(y[0], xa[z * 2]) + nt(y[1], xa[z * 2 + 1])

    def chunk(kind, k):
        return ds.at[kind, pl.ds(pl.multiple_of(zc(k) * CH, CH), CH)]

    def hops(kind, way):
        return HOPS[(kind + way) % 2]

    def send_sum(kind, way, t):
        n = hops(kind, way)
        sign = 1 - 2 * way
        mine = chunk(kind, -sign * (n - t))
        if t == 0:
            src = mine
        else:
            src = rb.at[kind, way, t - 1]
            landed(src, rs_r.at[kind, way, t - 1])
            src[...] = src[...] + mine[...]
        start(
            src, rb.at[kind, way, t], rs_s.at[kind, way, t], rs_r.at[kind, way, t],
            dev(zc(-sign), c, b),
        )

    landed(yo.at[oc], y_r.at[0])
    product(yo, 0)
    send_sum(0, 0, 0)
    send_sum(0, 1, 0)
    landed(yn.at[0], y_r.at[1])
    landed(yn.at[1], y_r.at[2])
    product(yn, 1)
    send_sum(1, 1, 0)
    send_sum(1, 0, 0)

    for k in range(1, NZ):
        landed(ga.at[zc(k)], ga_r.at[k])
    if upto == 4:
        for kind in range(2):
            for way in range(2):
                landed(rb.at[kind, way, 0], rs_r.at[kind, way, 0])
        stop()
        return

    gx = jnp.concatenate([ga[j] for j in range(NZ)], axis=1)
    total_sq = gx[SPARE:SPARE + 1, :]
    ones_row = gx[ONE:ONE + 1, :]
    inv = gm[:, 0:XR]
    centred = jnp.where(rowg < NC, gx - colmean * ones_row, 0.0)
    explained = jnp.sum(centred * mm(inv, centred, HIGH), axis=0, keepdims=True)
    weight = 1.0 / (jnp.maximum(total_sq - explained, 0.0) + EPS)
    beta_g = mm(inv, jnp.where((rowg < NC) | (rowg == ONE), gx, 0.0), HIGH)

    for t in range(1, 4):
        for kind, way in ((0, 0), (0, 1), (1, 1), (1, 0)):
            if t < hops(kind, way):
                send_sum(kind, way, t)

    at = b * VB + c * VH + lax.broadcasted_iota(jnp.int32, (CH, VH), 1)
    gene = lax.div(z, 2)

    def largest(kind, owner):
        total = chunk(kind, 0)[...]
        for way in range(2):
            last = hops(kind, way) - 1
            landed(rb.at[kind, way, last], rs_r.at[kind, way, last])
            total = total + rb[kind, way, last]
        numer = total[:, 0:VH] - mm(total[:, VH:VH + XR], beta_g, HIGH)
        first = win[0, owner * NG + gene]
        last = win[1, owner * NG + gene]
        inside = (at >= first) & (at < last)
        best = jnp.max(jnp.where(inside, numer * numer * weight, 0.0), axis=1, keepdims=True)
        return jnp.broadcast_to(best, (CH, 128))

    xs[0] = largest(0, b)
    start(xs.at[0], xm.at[0], x_s.at[0], x_r.at[0], dev(z, oc, b))
    xs[1] = largest(1, nbr)
    start(xs.at[1], xm.at[2 - c], x_s.at[1], x_r.at[2 - c], dev(z, c, nbr))
    start(xs.at[1], xm.at[2 - c], x_s.at[2], x_r.at[2 - c], dev(z, oc, nbr))
    for j in range(3):
        landed(xm.at[j], x_r.at[j])
    best = jnp.maximum(jnp.maximum(xs[0], xm[0]), jnp.maximum(xm[1], xm[2])) * float(NSAMP)

    r24 = lax.broadcasted_iota(jnp.int32, (CH, 128), 0)
    l24 = lax.broadcasted_iota(jnp.int32, (CH, 128), 1)
    peaks = jnp.sum(
        jnp.where(l24 == r24 + CH * lax.rem(z, 2), best, 0.0), axis=0, keepdims=True
    )
    level = LEVMAX * l24.astype(F32) / (LEVELS - 1)
    curve = jnp.sum(jax.nn.sigmoid(best - level), axis=0, keepdims=True)
    r8 = lax.broadcasted_iota(jnp.int32, (8, 128), 0)
    fm[z] = jnp.where(r8 == 0, peaks, jnp.where(r8 == 1, curve, 0.0))
    for k in range(1, NZ):
        start(fm.at[z], fm.at[z], f_s.at[k], f_r.at[NZ - k], dev(zc(k), c, b))
    for k in range(1, NZ):
        landed(fm.at[zc(k)], f_r.at[k])
    for g in range(NG):
        both = fm[2 * g] + fm[2 * g + 1]
        peak_ref[g:g + 1, :] = both[0:1, 0:NP]
        cur_ref[g:g + 1, :] = both[1:2, 0:LEVELS] * (1.0 / NP)
    finish()


def per_device(upto, geno, covar, pheno, perm, windows):
    dma = pltpu.SemaphoreType.DMA
    vmem = pltpu.VMEM
    spec = pl.BlockSpec(memory_space=pltpu.VMEM)
    return pl.pallas_call(
        functools.partial(kernel, upto),
        out_shape=(
            jax.ShapeDtypeStruct((NG, LEVELS), F32),
            jax.ShapeDtypeStruct((NG, NP), F32),
        ),
        in_specs=[
            pl.BlockSpec(memory_space=pl.ANY), spec, spec, spec,
            pl.BlockSpec(memory_space=pltpu.SMEM),
        ],
        out_specs=(spec, spec),
        scratch_shapes=[
            vmem((2 * NZ, XR, NS), BF16),
            vmem((8, NS), F32),
            vmem((2, NS, VH), BF16),
            vmem((NZ, XR, 128), F32),
            vmem((NZ, XR, 128), F32),
            vmem((NZ, XR, 128), F32),
            vmem((XR, 128), F32),
            vmem((2 * NZ, 8, NS), F32),
            vmem((2, ROWS, NS), BF16),
            vmem((2, ROWS, NS), BF16),
            vmem((2, ROWS, DW), F32),
            vmem((2, 2, 4, CH, DW), F32),
            vmem((2, CH, 128), F32),
            vmem((3, CH, 128), F32),
            vmem((NZ, 8, 128), F32),
            dma, dma, dma,
            dma((2, 4)), dma((2, 4)),
            dma((NZ,)), dma((NZ,)),
            dma((NZ,)), dma((NZ,)),
            dma((NZ,)), dma((NZ,)),
            dma((3,)), dma((3,)),
            dma((2, 2, 4)), dma((2, 2, 4)),
            dma((3,)), dma((3,)),
            dma((NZ,)), dma((NZ,)),
        ],
        compiler_params=pltpu.CompilerParams(
            collective_id=0, has_side_effects=True, vmem_limit_bytes=40 * 1024 * 1024
        ),
        name="scan",
    )(geno, covar.T, pheno.T, perm, windows.T)


def build(mesh, upto):
    in_specs = (P("samp", "var"), P("samp", None), P("samp", "var"), P(None, "samp"), P())
    out_specs = (P("var", None), P("var", None))
    return jax.shard_map(
        functools.partial(per_device, upto), mesh=mesh, in_specs=in_specs, out_specs=out_specs,
        check_vma=False,
    )


def solution(mesh):
    return build(mesh, 9)
```

time: 334 us -> 96.7 us (0.29)
  blocking collectives: 118 us -> 0 us
  Pallas kernels: 0 us -> 90 us
  local copies, waits for them, and re-layouts: 94.8 us -> 5.77 us
  waiting for transfers between devices: 70.7 us -> 0 us
  matrix products: 15.5 us -> 0 us
  between operations: 14.3 us -> 0.65 us
  other arithmetic: 9.13 us -> 0 us
  starting transfers between devices: 9.13 us -> 0 us
    gather x2 -> x0, local copies, waits for them, and re-layouts: 91.3 us -> none  [per_device(): shuffled = jnp.take(yall, perm, axis=0)]
    pallas_call x0 -> x1, Pallas kernels: none -> 90 us  [per_device(): pl.pallas_call(functools.partial(kernel, upto), out_shape=(jax.ShapeDtype...]
    psum x2 -> x0, blocking collectives: 72.8 us -> none  [the longest x1 48.8 us: per_device(): lax.psum((cross_part, ycross_part, gcross_part), 'samp')]
    reduce_scatter x1 -> x0, waiting for transfers between devices: 62.5 us -> none  [per_device(): lax.psum_scatter(direct - adjust, 'samp', scatter_dimension=0, tiled=True)]
    pmax x1 -> x0, blocking collectives: 27.2 us -> none  [per_device(): merged = lax.pmax(part_max, 'samp')]
    all_gather x1 -> x0, blocking collectives: 17.9 us -> none  [per_device(): yall = lax.all_gather(yres, 'samp', axis=0, tiled=True)]
    dot_general x8 -> x0, matrix products: 13.4 us -> none  [the longest x1 3.98 us: per_device(): lax.dot_general(beta_g, proj, (((0,), (0,)), ((), ())), precision=lax.Pre...]
    ppermute x4 -> x0, starting transfers between devices: 9.05 us -> none  [the longest x2 6.47 us: padded(): lax.ppermute(lax.slice_in_dim(block, block.shape[dim] - width, None, axis...]
  transfers between devices with their start and end apart: 6 -> 0, of which waited for: 4 -> 0; matrix products, arithmetic and copies ran while one was open for 31% -> 0% of each run, Pallas kernels for 0% -> 0%
where the time goes in v1:
time: 96.7 us; the launch traced here: 96.4 us
  Pallas kernels  90 us (93%)
  local copies, waits for them, and re-layouts  5.77 us (6%)
    pallas_call x1, Pallas kernels, per_device(): pl.pallas_call(functools.partial(kernel, upto), out_shape=(jax.ShapeDtype...  90 us
    unnamed x12, local copies, waits for them, and re-layouts  5.77 us

profile of v1, /device:TPU:1, one launch (start us, length us, event | category | flops | bytes accessed | tf_op | source)
XLA Modules:
  0.0 96.4 jit_solution(10515610697203153343)
XLA Ops:
  0.6 0.0 copy-start
  0.6 1.6 %copy-done = bf16[512,2048]{1,0:T(8,128)(2,1)S(1)} copy-done((bf16[512,2048]{1,0:T(8,128)(2,1)S(1)}, bf16[512,2048]{1,0:T(8,128)(2,1)}, u32[]{:S(2)}) %copy-start) | copy-done | bytes 2097176
  2.2 0.0 copy-start.1
  2.2 0.9 copy-done.1
  3.1 0.0 copy-start.2
  3.1 0.8 copy-done.2
  3.9 0.0 copy-start.3
  3.9 0.7 copy-done.3
  4.6 0.0 copy-start.4
  4.6 0.7 copy-done.4
  5.3 90.0 %scan.1 = (f32[4,64]{1,0:T(4,128)S(1)}, f32[4,48]{1,0:T(4,128)S(1)}) custom-call(bf16[512,2048]{1,0:T(8,128)(2,1)S(1)} %copy-done, bf16[32,512]{1,0:T(8,128)(2,1)S(1)} %bitcast.3, f32[4,512]{1,0:T(4,128)S(1)} %bitcast.4, s32[48,512]{1,0:T(8,128)S(1)} %copy-done.1, s32[2,64]{1,0:T(2,128)S(1)} %bitcast.5), custom_call_target="tpu_custom_call" | custom-call | tf_op jit(solution)/shard_map/scan/pallas_call | solution.py:408
  95.3 0.6 copy.9
  95.9 0.6 copy.10
Async XLA Ops:
  0.6 1.6 %copy-start = (bf16[512,2048]{1,0:T(8,128)(2,1)S(1)}, bf16[512,2048]{1,0:T(8,128)(2,1)}, u32[]{:S(2)}) copy-start(bf16[512,2048]{1,0:T(8,128)(2,1)} %geno.1) | copy-start | bytes 6291460
  2.2 0.9 copy-start.1
  3.1 0.8 copy-start.2
  3.9 0.7 copy-start.3
  4.6 0.7 copy-start.4

commit v2 on v0

v2 whole, which is shorter than its diff:
```python
import functools

import jax
import jax.numpy as jnp
from jax import lax
from jax.experimental import pallas as pl
from jax.experimental.pallas import tpu as pltpu
from jax.sharding import PartitionSpec as P

MESH = pl.DeviceIdType.MESH
F32 = jnp.float32
BF16 = jnp.bfloat16
HIGH = lax.Precision.HIGHEST

EPS = 1e-06
LEVMAX = 40.0
LEVELS = 64

NZ = 8
NB = 16
NS = 512
NSAMP = 8192
VB = 2048
VH = 1024
NG = 4
NP = 48
NC = 32
XR = 48
ONE = 44
SPARE = 45
GR = 40
GONE = 36
GSP = 37
ROWS = NG * NP
CH = ROWS // NZ
DW = VH + 128
HOPS = (4, 3)
LO = 256
TR = NSAMP // LO * NG
PZ = NP // NZ


def nt(a, b):
    return lax.dot_general(a, b, (((1,), (1,)), ((), ())), preferred_element_type=F32)


def mm(a, b, precision=None):
    return lax.dot_general(
        a, b, (((1,), (0,)), ((), ())), preferred_element_type=F32, precision=precision
    )


def iota(shape, dim):
    return lax.broadcasted_iota(jnp.int32, shape, dim)


def fold_rows(v):
    head, body, tail = v[0:32], v[32:40], v[40:48]
    low = iota(body.shape, 0) < 4
    return jnp.concatenate(
        [head, jnp.where(low, body + pltpu.roll(body, 4, axis=0) + tail, tail)], axis=0
    )


def kernel(
    upto,
    geno, covh, pheh, permh, winh,
    cur_ref, peak_ref,
    perm, win, xc, xy, xp, gs, gg, pk, gm, gcp, gr, ga, gh, yt, tab, yo, ds, rb, xs, xm, fm,
    in_sem, geno_sem, g1_s, g1_r, p_s, p_r, pk_s, pk_r, c_s, c_r, f_s, f_r, h_s, h_r,
    gr_s, gr_r, ga_s, ga_r, gh_s, gh_r, t_s, t_r, y_s, y_r, rs_s, rs_r, x_s, x_r, o_s, o_r,
):
    s = lax.axis_index("samp")
    b = lax.axis_index("var")
    z = lax.div(s, 2)
    c = lax.rem(s, 2)
    oc = 1 - c
    up_band = lax.rem(b + 1, NB)
    down_band = lax.rem(b + NB - 1, NB)
    nbr = lax.rem(b + 2 * c - 1 + NB, NB)
    own_at = pl.multiple_of(oc * VH, VH)
    halo_at = pl.multiple_of(c * VH, VH)

    def zc(k):
        return lax.rem(z + (k + NZ), NZ)

    def dev(zz, cc, bb):
        return {"samp": zz * 2 + cc, "var": bb}

    def half(cc):
        return pl.ds(pl.multiple_of(cc * VH, VH), VH)

    sent, due = [], {}

    def start(key, src, dst, ss, rs, to, here, here_sem):
        d = pltpu.make_async_remote_copy(
            src_ref=src, dst_ref=dst, send_sem=ss, recv_sem=rs, device_id=to, device_id_type=MESH
        )
        d.start()
        sent.append(d)
        due[key] = (here, here_sem)

    def landed(key):
        here, sem = due.pop(key)
        pltpu.make_async_remote_copy(
            src_ref=here, dst_ref=here, send_sem=sem, recv_sem=sem,
            device_id=dev(z, oc, b), device_id_type=MESH,
        ).wait_recv()

    def stop():
        for key in list(due):
            landed(key)
        for d in sent:
            d.wait_send()

    def cut(level):
        if upto != level:
            return False
        stop()
        cur_ref[...] = jnp.zeros_like(cur_ref)
        peak_ref[...] = jnp.zeros_like(peak_ref)
        return True

    other = dev(z, oc, b)
    loads = [
        pltpu.make_async_copy(src, dst, in_sem.at[i])
        for i, (src, dst) in enumerate((
            (covh, xc.at[z]), (pheh, xy.at[z]), (permh, perm), (winh, win),
        ))
    ]
    for d in loads:
        d.start()
    barrier = pltpu.get_barrier_semaphore()
    peers = [dev(zc(k), c, b) for k in range(1, NZ)] + [other]
    peers += [dev(z, cc, bb) for cc in (0, 1) for bb in (up_band, down_band)]
    for peer in peers:
        pl.semaphore_signal(barrier, inc=1, device_id=peer, device_id_type=MESH)
    own_geno = pltpu.make_async_copy(geno.at[:, half(c)], gs.at[c, :, pl.ds(own_at, VH)], geno_sem)
    own_geno.start()
    for d in loads:
        d.wait()

    phe = xy[z]
    full = jnp.concatenate([phe, phe], axis=0)
    hi = full.astype(BF16).astype(F32)
    rest = full - hi
    mid = rest.astype(BF16).astype(F32)
    low = (rest - mid).astype(BF16).astype(F32)
    row8 = iota((8, NS), 0)
    block_a = jnp.where(row8 < 4, hi, mid)
    block_b = jnp.where(row8 < 4, low, jnp.where(row8 == 4, 1.0, 0.0))
    xp[c] = jnp.concatenate([xc[z].astype(F32), block_a, block_b], axis=0).astype(BF16)
    mine = xp[c]
    gg[c] = jnp.zeros((GR, 128), F32)
    gg[c, :, 0:XR] = fold_rows(nt(mine, mine))

    pl.semaphore_wait(barrier, len(peers))
    start("g1", gg.at[c], gg.at[c], g1_s, g1_r, other, gg.at[oc], g1_r)
    start("p", xp.at[c], xp.at[c], p_s, p_r, other, xp.at[oc], p_r)
    if cut(0):
        own_geno.wait()
        return

    landed("g1")
    g = gg[0] + gg[1]
    lane40 = iota((GR, 128), 1)
    g = jnp.where(lane40 < GONE, g, pltpu.roll(g, 128 - (ONE - GONE), axis=1))
    g = jnp.concatenate([g, jnp.zeros((8, 128), F32)], axis=0)
    lane16 = iota((16, 128), 1)
    pk[z] = jnp.where(
        lane16 < GR, g[0:16],
        jnp.where(lane16 < 2 * GR, pltpu.roll(g[16:32], GR, axis=1),
                  jnp.where(lane16 < 3 * GR, pltpu.roll(g[32:48], 2 * GR, axis=1), 0.0)),
    )
    near = (1, 7, 2, 6, 3, 5, 4)
    for k in near:
        start(("pk", k), pk.at[z], pk.at[z], pk_s.at[k], pk_r.at[NZ - k], dev(zc(k), c, b),
              pk.at[zc(k)], pk_r.at[k])
    start("f", geno.at[:, half(oc)], gs.at[c, :, half(c)], f_s, f_r, other,
          gs.at[oc, :, pl.ds(own_at, VH)], f_r)
    for k in near:
        to = dev(zc(k), c, b)
        start(("c", k), xc.at[z], xc.at[z], c_s.at[0, k], c_r.at[0, NZ - k], to,
              xc.at[zc(k)], c_r.at[0, k])
        start(("y", k), xy.at[z], xy.at[z], c_s.at[1, k], c_r.at[1, NZ - k], to,
              xy.at[zc(k)], c_r.at[1, k])
    halo = gs.at[0, :, pl.ds(halo_at, VH)], gs.at[1, :, pl.ds(halo_at, VH)]
    start("h0", geno.at[:, VH:2 * VH], gs.at[c, :, 0:VH], h_s.at[0], h_r.at[c],
          dev(z, 0, up_band), halo[0], h_r.at[0])
    start("h1", geno.at[:, 0:VH], gs.at[c, :, VH:2 * VH], h_s.at[1], h_r.at[c],
          dev(z, 1, down_band), halo[1], h_r.at[1])

    own_geno.wait()
    landed("f")
    landed("p")
    gpart = fold_rows(
        mm(xp[0], gs[0, :, pl.ds(own_at, VH)]) + mm(xp[1], gs[1, :, pl.ds(own_at, VH)])
    )
    mean = gpart[GONE:GONE + 1, :] * (1.0 / (2 * NS))

    def spread(i, acc):
        at = pl.ds(pl.multiple_of(lax.rem(i, 32) * 16, 16), 16)
        dif = gs[lax.div(i, 32), at, pl.ds(own_at, VH)].astype(F32) - mean
        return acc + dif * dif

    acc = lax.fori_loop(0, 64, spread, jnp.zeros((16, VH), F32))
    rowg = iota((GR, VH), 0)
    gpart = jnp.where(rowg == GSP, jnp.sum(acc, axis=0, keepdims=True), gpart)
    for j in range(NZ):
        gcp[j] = gpart[:, j * 128:(j + 1) * 128]

    for k in range(1, NZ):
        landed(("pk", k))
    if cut(1):
        return
    tot = pk[0]
    for j in range(1, NZ):
        tot = tot + pk[j]
    a = jnp.concatenate(
        [tot, pltpu.roll(tot, 128 - GR, axis=1), pltpu.roll(tot, 128 - 2 * GR, axis=1)[0:8]], axis=0
    )
    row, lane = iota((GR, 128), 0), iota((GR, 128), 1)
    in_row = (row < NC) | (row == GONE)
    in_lane = (lane < NC) | (lane == GONE)
    a = jnp.where(in_lane, a, 0.0)
    colmean = a[:, GONE:GONE + 1] * (1.0 / NSAMP)
    for k in (GONE,) + tuple(range(NC)):
        q = a[:, k:k + 1]
        r = a[k:k + 1, :]
        inv = 1.0 / a[k:k + 1, k:k + 1]
        rr = r * inv
        nxt = a - q * rr
        nxt = jnp.where(row == k, rr, nxt)
        nxt = jnp.where(lane == k, jnp.where(row == k, -inv, q * inv), nxt)
        a = nxt
    gm[...] = jnp.where(in_row & in_lane, -a, 0.0)
    for k in near:
        start(("gr", k), gcp.at[zc(k)], gr.at[z], gr_s.at[k], gr_r.at[NZ - k], dev(zc(k), c, b),
              gr.at[zc(k)], gr_r.at[k])

    beta = a[32:40, :]
    row24 = beta.astype(BF16).astype(F32)
    rest = beta - row24
    mid = rest.astype(BF16).astype(F32)
    coefs = jnp.concatenate([row24, mid, rest - mid], axis=0)[:, 0:NC].astype(BF16)
    const = beta[0:4, GONE:GONE + 1]
    if cut(2):
        return
    for k in (0,) + near:
        if k:
            landed(("c", k))
            landed(("y", k))
        t = mm(coefs, xc[zc(k)])
        fit = (t[16:24] + t[8:16]) + t[0:8]
        yt[c, zc(k)] = xy[zc(k)] - (fit[0:4] + const)
    start("t", yt.at[c], yt.at[c], t_s, t_r, other, yt.at[oc], t_r)

    for k in range(1, NZ):
        landed(("gr", k))
    gr[z] = gcp[z]
    tot = gr[0]
    for j in range(1, NZ):
        tot = tot + gr[j]
    mu = tot[GONE:GONE + 1, :] * (1.0 / NSAMP)
    between = jnp.zeros((1, 128), F32)
    for j in range(NZ):
        off = gr[j, GONE:GONE + 1, :] * (1.0 / (2 * NS)) - mu
        between = between + off * off
    ga[z] = tot + jnp.where(row == GSP, between * (2.0 * NS), 0.0)
    for k in near:
        start(("ga", k), ga.at[z], ga.at[z], ga_s.at[k], ga_r.at[NZ - k], dev(zc(k), c, b),
              ga.at[zc(k)], ga_r.at[k])

    landed("t")
    ysq = jnp.zeros((NG, NS), F32)
    for cc in range(2):
        for j in range(NZ):
            ysq = ysq + yt[cc, j] * yt[cc, j]
    ynorm = jnp.sqrt(jnp.sum(ysq, axis=1, keepdims=True) + EPS)
    for cc in range(2):
        for j in range(NZ):
            y = yt[cc, j] / ynorm
            for q in range(2):
                at = (2 * (2 * j + cc) + q) * NG
                tab[at:at + NG, :] = y[:, q * LO:(q + 1) * LO]
    if cut(3):
        return

    table = tab[...].astype(BF16)
    count = iota((LO, NS), 0).astype(F32).astype(BF16)
    holds = lax.shift_right_logical(iota((TR, NS), 0), 2)
    low_half = iota((8, NS), 0) < NG
    one = jnp.ones((), BF16)
    zero = jnp.zeros((), BF16)

    def look(i, carry):
        got = []
        for u in range(4):
            idx = perm[pl.ds(i * 4 + u, 1), :]
            ilo = lax.bitwise_and(idx, LO - 1).astype(F32).astype(BF16)
            found = mm(table, jnp.where(count == ilo, one, zero))
            found = jnp.where(holds == lax.shift_right_logical(idx, 8), found, 0.0)
            part = found[0:8]
            for j in range(1, TR // 8):
                part = part + found[j * 8:(j + 1) * 8]
            got.append(part + pltpu.roll(part, NG, axis=0))
        rows = jnp.concatenate(
            [jnp.where(low_half, got[0], got[1]), jnp.where(low_half, got[2], got[3])], axis=0
        )
        yo[c, pl.ds(pl.multiple_of(i * 16, 16), 16), :] = rows.astype(BF16)
        return carry

    for j in range(3):
        lax.fori_loop(j * 4, j * 4 + 4, look, 0)
        part = pl.ds(j * 64, 64)
        start(("yo", j), yo.at[c, part], yo.at[c, part], y_s.at[j], y_r.at[j], other,
              yo.at[oc, part], y_r.at[j])
    if cut(4):
        return
    for j in range(3):
        landed(("yo", j))

    def product(kind, at):
        ds[kind, :, 0:VH] = mm(yo[0], gs[0, :, pl.ds(at, VH)]) + mm(yo[1], gs[1, :, pl.ds(at, VH)])

    def chunk(kind, k):
        return ds.at[kind, pl.ds(pl.multiple_of(zc(k) * CH, CH), CH)]

    def hops(kind, way):
        return HOPS[(kind + way) % 2]

    def send_sum(kind, way, t):
        n = hops(kind, way)
        sign = 1 - 2 * way
        mine = chunk(kind, -sign * (n - t))
        if t == 0:
            src = mine
        else:
            src = rb.at[kind, way, t - 1]
            landed(("rs", kind, way, t - 1))
            src[...] = src[...] + mine[...]
        start(
            ("rs", kind, way, t), src, rb.at[kind, way, t], rs_s.at[kind, way, t],
            rs_r.at[kind, way, t], dev(zc(-sign), c, b),
            rb.at[kind, way, t], rs_r.at[kind, way, t],
        )

    ds[0, :, VH:DW] = jnp.zeros((ROWS, 128), F32)
    ds[1, :, VH:DW] = jnp.zeros((ROWS, 128), F32)
    ds[0, :, VH:VH + XR] = nt(yo[0], xp[0]) + nt(yo[1], xp[1])
    product(0, own_at)
    send_sum(0, 0, 0)
    send_sum(0, 1, 0)
    landed("h0")
    landed("h1")
    product(1, halo_at)
    send_sum(1, 1, 0)
    send_sum(1, 0, 0)
    if cut(5):
        return

    for k in range(1, NZ):
        landed(("ga", k))
    start("gh", ga, gh, gh_s, gh_r, dev(z, oc, nbr), gh, gh_r)

    inv = gm[:, 0:GR]

    def of_variants(ref):
        gx = jnp.concatenate([ref[j] for j in range(NZ)], axis=1)
        centred = jnp.where(rowg < NC, gx - colmean * gx[GONE:GONE + 1, :], 0.0)
        explained = jnp.sum(centred * mm(inv, centred, HIGH), axis=0, keepdims=True)
        weight = 1.0 / (jnp.maximum(gx[GSP:GSP + 1, :] - explained, 0.0) + EPS)
        return mm(inv, jnp.where((rowg < NC) | (rowg == GONE), gx, 0.0), HIGH), weight

    beta_own, weight_own = of_variants(ga)
    order = ((0, 0), (0, 1), (1, 1), (1, 0))
    for kind, way in order:
        send_sum(kind, way, 1)
    landed("gh")
    beta_halo, weight_halo = of_variants(gh)
    for t in range(2, 4):
        for kind, way in order:
            if t < hops(kind, way):
                send_sum(kind, way, t)

    gene24 = lax.rem(iota((CH, 1), 0), NG)
    first = jnp.zeros((CH, 1), jnp.int32)
    last = jnp.zeros((CH, 1), jnp.int32)
    for g in range(NG):
        first = jnp.where(gene24 == g, win[0, b * NG + g], first)
        last = jnp.where(gene24 == g, win[1, b * NG + g], last)
    base = b * VB - VH + c * VB + iota((CH, VH), 1)

    sums = []
    for kind in range(2):
        total = chunk(kind, 0)[...]
        for way in range(2):
            end = hops(kind, way) - 1
            landed(("rs", kind, way, end))
            total = total + rb[kind, way, end]
        sums.append(total)
    if cut(6):
        return
    proj = jnp.where(iota((CH, XR), 1) < 32, sums[0][:, VH:VH + XR], 0.0)
    l48 = iota((CH, XR), 1)
    proj = jnp.where(l48 == GONE, sums[0][:, VH + ONE:VH + ONE + 1], proj)[:, 0:GR]

    def largest(kind, at, beta_g, weight):
        numer = sums[kind][:, 0:VH] - mm(proj, beta_g, HIGH)
        pos = base + at
        inside = (pos >= first) & (pos < last)
        return jnp.max(jnp.where(inside, numer * numer * weight, 0.0), axis=1, keepdims=True)

    best = jnp.maximum(
        largest(0, own_at, beta_own, weight_own), largest(1, halo_at, beta_halo, weight_halo)
    )
    xs[...] = jnp.broadcast_to(best, (CH, 128))
    start("x", xs, xm, x_s, x_r, other, xm, x_r)
    landed("x")
    best = jnp.maximum(xs[...], xm[...]) * float(NSAMP)

    r24, l24 = iota((CH, 128), 0), iota((CH, 128), 1)
    placed = jnp.where(l24 == lax.shift_right_logical(r24, 2) + PZ * z, best, 0.0)
    level = LEVMAX * l24.astype(F32) / (LEVELS - 1)
    curve = jax.nn.sigmoid(best - level)

    def over_perms(v):
        v = (v[0:8] + v[8:16]) + v[16:24]
        return v + pltpu.roll(v, NG, axis=0)

    fm[z] = jnp.where(iota((8, 128), 0) < NG, over_perms(placed), over_perms(curve))
    for k in near:
        start(("o", k), fm.at[z], fm.at[z], o_s.at[k], o_r.at[NZ - k], dev(zc(k), c, b),
              fm.at[zc(k)], o_r.at[k])
    for k in range(1, NZ):
        landed(("o", k))
    both = fm[0]
    for j in range(1, NZ):
        both = both + fm[j]
    peak_ref[...] = both[0:NG, 0:NP]
    cur_ref[...] = both[NG:2 * NG, 0:LEVELS] * (1.0 / NP)
    stop()


def per_device(upto, geno, covar, pheno, perm, windows):
    dma = pltpu.SemaphoreType.DMA
    vmem = pltpu.VMEM
    spec = pl.BlockSpec(memory_space=pltpu.VMEM)
    return pl.pallas_call(
        functools.partial(kernel, upto),
        out_shape=(
            jax.ShapeDtypeStruct((NG, LEVELS), F32),
            jax.ShapeDtypeStruct((NG, NP), F32),
        ),
        in_specs=[pl.BlockSpec(memory_space=pltpu.HBM)] * 5,
        out_specs=(spec, spec),
        scratch_shapes=[
            vmem((NP, NS), jnp.int32),
            pltpu.SMEM((2, NG * NB), jnp.int32),
            vmem((NZ, NC, NS), BF16),
            vmem((NZ, NG, NS), F32),
            vmem((2, XR, NS), BF16),
            vmem((2, NS, VB), BF16),
            vmem((2, GR, 128), F32),
            vmem((NZ, 16, 128), F32),
            vmem((GR, 128), F32),
            vmem((NZ, GR, 128), F32),
            vmem((NZ, GR, 128), F32),
            vmem((NZ, GR, 128), F32),
            vmem((NZ, GR, 128), F32),
            vmem((2, NZ, NG, NS), F32),
            vmem((TR, LO), F32),
            vmem((2, ROWS, NS), BF16),
            vmem((2, ROWS, DW), F32),
            vmem((2, 2, 4, CH, DW), F32),
            vmem((CH, 128), F32),
            vmem((CH, 128), F32),
            vmem((NZ, 8, 128), F32),
            dma((4,)), dma,
            dma, dma, dma, dma,
            dma((NZ,)), dma((NZ,)),
            dma((2, NZ)), dma((2, NZ)),
            dma, dma,
            dma((2,)), dma((2,)),
            dma((NZ,)), dma((NZ,)),
            dma((NZ,)), dma((NZ,)),
            dma, dma, dma, dma,
            dma((3,)), dma((3,)),
            dma((2, 2, 4)), dma((2, 2, 4)),
            dma, dma,
            dma((NZ,)), dma((NZ,)),
        ],
        compiler_params=pltpu.CompilerParams(
            collective_id=0, has_side_effects=True, vmem_limit_bytes=56 * 1024 * 1024
        ),
        name="scan",
    )(geno, covar.T, pheno.T, perm, windows.T)


def build(mesh, upto):
    in_specs = (P("samp", "var"), P("samp", None), P("samp", "var"), P(None, "samp"), P())
    out_specs = (P("var", None), P("var", None))
    return jax.shard_map(
        functools.partial(per_device, upto), mesh=mesh, in_specs=in_specs, out_specs=out_specs,
        check_vma=False,
    )


def solution(mesh):
    return build(mesh, 9)
```

time: 334 us -> 67.6 us (0.20)
  blocking collectives: 118 us -> 0 us
  local copies, waits for them, and re-layouts: 94.8 us -> 2.48 us
  waiting for transfers between devices: 70.7 us -> 0 us
  Pallas kernels: 0 us -> 64.3 us
  matrix products: 15.5 us -> 0 us
  between operations: 14.3 us -> 0.64 us
  other arithmetic: 9.13 us -> 0 us
  starting transfers between devices: 9.13 us -> 0 us
    gather x2 -> x0, local copies, waits for them, and re-layouts: 91.3 us -> none  [per_device(): shuffled = jnp.take(yall, perm, axis=0)]
    psum x2 -> x0, blocking collectives: 72.8 us -> none  [the longest x1 48.8 us: per_device(): lax.psum((cross_part, ycross_part, gcross_part), 'samp')]
    pallas_call x0 -> x1, Pallas kernels: none -> 64.3 us  [per_device(): pl.pallas_call(functools.partial(kernel, upto), out_shape=(jax.ShapeDtype...]
    reduce_scatter x1 -> x0, waiting for transfers between devices: 62.5 us -> none  [per_device(): lax.psum_scatter(direct - adjust, 'samp', scatter_dimension=0, tiled=True)]
    pmax x1 -> x0, blocking collectives: 27.2 us -> none  [per_device(): merged = lax.pmax(part_max, 'samp')]
    all_gather x1 -> x0, blocking collectives: 17.9 us -> none  [per_device(): yall = lax.all_gather(yres, 'samp', axis=0, tiled=True)]
    dot_general x8 -> x0, matrix products: 13.4 us -> none  [the longest x1 3.98 us: per_device(): lax.dot_general(beta_g, proj, (((0,), (0,)), ((), ())), precision=lax.Pre...]
    ppermute x4 -> x0, starting transfers between devices: 9.05 us -> none  [the longest x2 6.47 us: padded(): lax.ppermute(lax.slice_in_dim(block, block.shape[dim] - width, None, axis...]
  transfers between devices with their start and end apart: 6 -> 0, of which waited for: 4 -> 0; matrix products, arithmetic and copies ran while one was open for 31% -> 0% of each run, Pallas kernels for 0% -> 0%
where the time goes in v2:
time: 67.6 us; the launch traced here: 67.4 us
  Pallas kernels  64.3 us (95%)
  local copies, waits for them, and re-layouts  2.48 us (4%)
    pallas_call x1, Pallas kernels, per_device(): pl.pallas_call(functools.partial(kernel, upto), out_shape=(jax.ShapeDtype...  64.3 us
    unnamed x2, local copies, waits for them, and re-layouts  2.48 us

profile of v2, /device:TPU:1, one launch (start us, length us, event | category | flops | bytes accessed | tf_op | source)
XLA Modules:
  0.0 67.4 jit_solution(7097620380176221137)
XLA Ops:
  0.6 64.3 %scan.1 = (f32[4,64]{1,0:T(4,128)}, f32[4,48]{1,0:T(4,128)}) custom-call(bf16[512,2048]{1,0:T(8,128)(2,1)} %geno.1, bf16[32,512]{1,0:T(8,128)(2,1)} %bitcast.3, f32[4,512]{1,0:T(4,128)} %bitcast.4, s32[48,512]{1,0:T(8,128)} %permh.1, s32[2,64]{1,0:T(2,128)} %bitcast.5), custom_call_target="tpu_custom_call" | custom-call | tf_op jit(solution)/shard_map/scan/pallas_call | solution.py:449
  64.9 1.2 %copy.9 = f32[4,64]{1,0:T(4,128)} copy(f32[4,64]{1,0:T(4,128)} %get-tuple-element.4) | data formatting | bytes 2048
  66.2 1.2 %copy.10 = f32[4,48]{1,0:T(4,128)} copy(f32[4,48]{1,0:T(4,128)} %get-tuple-element.5) | data formatting | bytes 1536

commit v3 on v2

--- a/solution.py
+++ b/solution.py
@@ -33,7 +33,9 @@
 GSP = 37
 ROWS = NG * NP
 CH = ROWS // NZ
-DW = VH + 128
+HW = VH // 2
+QMAX = 32767.0
+TINY = 1e-30
 HOPS = (4, 3)
 LO = 256
 TR = NSAMP // LO * NG
@@ -66,9 +68,11 @@
     upto,
     geno, covh, pheh, permh, winh,
     cur_ref, peak_ref,
-    perm, win, xc, xy, xp, gs, gg, pk, gm, gcp, gr, ga, gh, yt, tab, yo, ds, rb, xs, xm, fm,
+    perm, win, xc, xy, xp, gs, gg, pk, gm, gcp, gr, ga, gh, yt, tab, yo, ds,
+    pq, pr, q0, s0, rb, sb, xs, xm, fm,
     in_sem, geno_sem, g1_s, g1_r, p_s, p_r, pk_s, pk_r, c_s, c_r, f_s, f_r, h_s, h_r,
-    gr_s, gr_r, ga_s, ga_r, gh_s, gh_r, t_s, t_r, y_s, y_r, rs_s, rs_r, x_s, x_r, o_s, o_r,
+    gr_s, gr_r, ga_s, ga_r, gh_s, gh_r, t_s, t_r, y_s, y_r,
+    pr_s, pr_r, rs_s, rs_r, x_s, x_r, o_s, o_r,
 ):
     s = lax.axis_index("samp")
     b = lax.axis_index("var")
@@ -82,7 +86,7 @@
     halo_at = pl.multiple_of(c * VH, VH)
 
     def zc(k):
-        return lax.rem(z + (k + NZ), NZ)
+        return lax.rem(z + k % NZ, NZ)
 
     def dev(zz, cc, bb):
         return {"samp": zz * 2 + cc, "var": bb}
@@ -178,12 +182,16 @@
               pk.at[zc(k)], pk_r.at[k])
     start("f", geno.at[:, half(oc)], gs.at[c, :, half(c)], f_s, f_r, other,
           gs.at[oc, :, pl.ds(own_at, VH)], f_r)
-    for k in near:
-        to = dev(zc(k), c, b)
-        start(("c", k), xc.at[z], xc.at[z], c_s.at[0, k], c_r.at[0, NZ - k], to,
-              xc.at[zc(k)], c_r.at[0, k])
-        start(("y", k), xy.at[z], xy.at[z], c_s.at[1, k], c_r.at[1, NZ - k], to,
-              xy.at[zc(k)], c_r.at[1, k])
+
+    def share(name, held, to):
+        ref = (xc, xy)[name == "y"]
+        i, k, got = int(name == "y"), (held - to) % NZ, zc(held - to)
+        start((name, k), ref.at[zc(held)], ref.at[zc(held)], c_s.at[i, k], c_r.at[i, k],
+              dev(zc(to), c, b), ref.at[got], c_r.at[i, k])
+
+    for to in (1, -1, 2, -2):
+        share("c", 0, to)
+        share("y", 0, to)
     halo = gs.at[0, :, pl.ds(halo_at, VH)], gs.at[1, :, pl.ds(halo_at, VH)]
     start("h0", geno.at[:, VH:2 * VH], gs.at[c, :, 0:VH], h_s.at[0], h_r.at[c],
           dev(z, 0, up_band), halo[0], h_r.at[0])
@@ -196,6 +204,14 @@
     gpart = fold_rows(
         mm(xp[0], gs[0, :, pl.ds(own_at, VH)]) + mm(xp[1], gs[1, :, pl.ds(own_at, VH)])
     )
+    for name in ("c", "y"):
+        for k in (6, 2):
+            landed((name, k))
+    share("c", -2, 2)
+    share("y", 2, -2)
+    for name in ("c", "y"):
+        share(name, -2, 1)
+        share(name, 2, -1)
     mean = gpart[GONE:GONE + 1, :] * (1.0 / (2 * NS))
 
     def spread(i, acc):
@@ -208,6 +224,9 @@
     gpart = jnp.where(rowg == GSP, jnp.sum(acc, axis=0, keepdims=True), gpart)
     for j in range(NZ):
         gcp[j] = gpart[:, j * 128:(j + 1) * 128]
+    for k in near:
+        start(("gr", k), gcp.at[zc(k)], gr.at[z], gr_s.at[k], gr_r.at[NZ - k], dev(zc(k), c, b),
+              gr.at[zc(k)], gr_r.at[k])
 
     for k in range(1, NZ):
         landed(("pk", k))
@@ -234,9 +253,6 @@
         nxt = jnp.where(lane == k, jnp.where(row == k, -inv, q * inv), nxt)
         a = nxt
     gm[...] = jnp.where(in_row & in_lane, -a, 0.0)
-    for k in near:
-        start(("gr", k), gcp.at[zc(k)], gr.at[z], gr_s.at[k], gr_r.at[NZ - k], dev(zc(k), c, b),
-              gr.at[zc(k)], gr_r.at[k])
 
     beta = a[32:40, :]
     row24 = beta.astype(BF16).astype(F32)
@@ -246,30 +262,14 @@
     const = beta[0:4, GONE:GONE + 1]
     if cut(2):
         return
-    for k in (0,) + near:
-        if k:
-            landed(("c", k))
-            landed(("y", k))
+    for k in (0, 7, 1, 6, 2, 5, 3, 4):
+        for name in ("c", "y"):
+            if (name, k) in due:
+                landed((name, k))
         t = mm(coefs, xc[zc(k)])
         fit = (t[16:24] + t[8:16]) + t[0:8]
         yt[c, zc(k)] = xy[zc(k)] - (fit[0:4] + const)
     start("t", yt.at[c], yt.at[c], t_s, t_r, other, yt.at[oc], t_r)
-
-    for k in range(1, NZ):
-        landed(("gr", k))
-    gr[z] = gcp[z]
-    tot = gr[0]
-    for j in range(1, NZ):
-        tot = tot + gr[j]
-    mu = tot[GONE:GONE + 1, :] * (1.0 / NSAMP)
-    between = jnp.zeros((1, 128), F32)
-    for j in range(NZ):
-        off = gr[j, GONE:GONE + 1, :] * (1.0 / (2 * NS)) - mu
-        between = between + off * off
-    ga[z] = tot + jnp.where(row == GSP, between * (2.0 * NS), 0.0)
-    for k in near:
-        start(("ga", k), ga.at[z], ga.at[z], ga_s.at[k], ga_r.at[NZ - k], dev(zc(k), c, b),
-              ga.at[zc(k)], ga_r.at[k])
 
     landed("t")
     ysq = jnp.zeros((NG, NS), F32)
@@ -310,44 +310,87 @@
         yo[c, pl.ds(pl.multiple_of(i * 16, 16), 16), :] = rows.astype(BF16)
         return carry
 
+    def sum_variants():
+        for k in range(1, NZ):
+            landed(("gr", k))
+        gr[z] = gcp[z]
+        tot = gr[0]
+        for j in range(1, NZ):
+            tot = tot + gr[j]
+        mu = tot[GONE:GONE + 1, :] * (1.0 / NSAMP)
+        between = jnp.zeros((1, 128), F32)
+        for j in range(NZ):
+            off = gr[j, GONE:GONE + 1, :] * (1.0 / (2 * NS)) - mu
+            between = between + off * off
+        ga[z] = tot + jnp.where(row == GSP, between * (2.0 * NS), 0.0)
+        for k in near:
+            start(("ga", k), ga.at[z], ga.at[z], ga_s.at[k], ga_r.at[NZ - k], dev(zc(k), c, b),
+                  ga.at[zc(k)], ga_r.at[k])
+
     for j in range(3):
         lax.fori_loop(j * 4, j * 4 + 4, look, 0)
         part = pl.ds(j * 64, 64)
         start(("yo", j), yo.at[c, part], yo.at[c, part], y_s.at[j], y_r.at[j], other,
               yo.at[oc, part], y_r.at[j])
+        if j == 0:
+            sum_variants()
     if cut(4):
         return
     for j in range(3):
         landed(("yo", j))
 
     def product(kind, at):
-        ds[kind, :, 0:VH] = mm(yo[0], gs[0, :, pl.ds(at, VH)]) + mm(yo[1], gs[1, :, pl.ds(at, VH)])
+        ds[kind] = mm(yo[0], gs[0, :, pl.ds(at, VH)]) + mm(yo[1], gs[1, :, pl.ds(at, VH)])
 
     def chunk(kind, k):
         return ds.at[kind, pl.ds(pl.multiple_of(zc(k) * CH, CH), CH)]
 
     def hops(kind, way):
         return HOPS[(kind + way) % 2]
+
+    def unpack(ref, scale):
+        q = ref[...].astype(F32)
+        return [q[CH * h:CH * (h + 1)] * scale[h:h + 1, :] for h in range(2)]
+
+    def halves(ref):
+        return [ref[:, HW * h:HW * (h + 1)] for h in range(2)]
 
     def send_sum(kind, way, t):
         n = hops(kind, way)
         sign = 1 - 2 * way
-        mine = chunk(kind, -sign * (n - t))
+        parts = halves(chunk(kind, -sign * (n - t)))
         if t == 0:
-            src = mine
+            src, scale = q0.at[kind, way], s0.at[kind, way]
         else:
-            src = rb.at[kind, way, t - 1]
+            src, scale = rb.at[kind, way, t - 1], sb.at[kind, way, t - 1]
             landed(("rs", kind, way, t - 1))
-            src[...] = src[...] + mine[...]
-        start(
-            ("rs", kind, way, t), src, rb.at[kind, way, t], rs_s.at[kind, way, t],
-            rs_r.at[kind, way, t], dev(zc(-sign), c, b),
-            rb.at[kind, way, t], rs_r.at[kind, way, t],
+            landed(("sc", kind, way, t - 1))
+            parts = [u + v for u, v in zip(parts, unpack(src, scale))]
+        codes = []
+        for h in range(2):
+            top = jnp.max(jnp.abs(parts[h]), axis=0, keepdims=True)
+            top = jnp.maximum(top, TINY)
+            scale[h:h + 1, :] = top * (1.0 / QMAX)
+            codes.append(jnp.round(parts[h] * (QMAX / top)))
+        src[...] = jnp.concatenate(codes, axis=0).astype(jnp.int32).astype(jnp.int16)
+        to = dev(zc(-sign), c, b)
+        for i, (name, here, buf) in enumerate((("rs", src, rb), ("sc", scale, sb))):
+            land = buf.at[kind, way, t]
+            start((name, kind, way, t), here, land, rs_s.at[i, kind, way, t],
+                  rs_r.at[i, kind, way, t], to, land, rs_r.at[i, kind, way, t])
+
+    proj = jnp.concatenate(
+        [nt(yo[0], xp[0]) + nt(yo[1], xp[1]), jnp.zeros((ROWS, 128 - XR), F32)], axis=1
+    )
+    proj = jnp.where(iota((ROWS, 128), 1) < GONE, proj, pltpu.roll(proj, 128 - (ONE - GONE), axis=1))
+    lane8 = iota((8, 128), 1)
+    for j in range(NZ):
+        p3 = [proj[CH * j + 8 * i:CH * j + 8 * i + 8] for i in range(3)]
+        pq[j] = jnp.where(
+            lane8 < GR, p3[0],
+            jnp.where(lane8 < 2 * GR, pltpu.roll(p3[1], GR, axis=1),
+                      pltpu.roll(p3[2], 2 * GR, axis=1)),
         )
-
-    ds[0, :, VH:DW] = jnp.zeros((ROWS, 128), F32)
-    ds[1, :, VH:DW] = jnp.zeros((ROWS, 128), F32)
-    ds[0, :, VH:VH + XR] = nt(yo[0], xp[0]) + nt(yo[1], xp[1])
     product(0, own_at)
     send_sum(0, 0, 0)
     send_sum(0, 1, 0)
@@ -356,6 +399,9 @@
     product(1, halo_at)
     send_sum(1, 1, 0)
     send_sum(1, 0, 0)
+    for k in near:
+        start(("pr", k), pq.at[zc(k)], pr.at[z], pr_s.at[k], pr_r.at[NZ - k], dev(zc(k), c, b),
+              pr.at[zc(k)], pr_r.at[k])
     if cut(5):
         return
 
@@ -391,22 +437,33 @@
         last = jnp.where(gene24 == g, win[1, b * NG + g], last)
     base = b * VB - VH + c * VB + iota((CH, VH), 1)
 
+    for k in range(1, NZ):
+        landed(("pr", k))
+    pr[z] = pq[z]
+    tot = pr[0]
+    for j in range(1, NZ):
+        tot = tot + pr[j]
+    proj = jnp.concatenate(
+        [tot, pltpu.roll(tot, 128 - GR, axis=1), pltpu.roll(tot, 128 - 2 * GR, axis=1)], axis=0
+    )
+    l24 = iota((CH, 128), 1)
+    proj = jnp.where((l24 < NC) | (l24 == GONE), proj, 0.0)[:, 0:GR]
+
     sums = []
     for kind in range(2):
-        total = chunk(kind, 0)[...]
+        parts = halves(chunk(kind, 0))
         for way in range(2):
             end = hops(kind, way) - 1
             landed(("rs", kind, way, end))
-            total = total + rb[kind, way, end]
-        sums.append(total)
+            landed(("sc", kind, way, end))
+            got = unpack(rb.at[kind, way, end], sb.at[kind, way, end])
+            parts = [u + v for u, v in zip(parts, got)]
+        sums.append(jnp.concatenate(parts, axis=1))
     if cut(6):
         return
-    proj = jnp.where(iota((CH, XR), 1) < 32, sums[0][:, VH:VH + XR], 0.0)
-    l48 = iota((CH, XR), 1)
-    proj = jnp.where(l48 == GONE, sums[0][:, VH + ONE:VH + ONE + 1], proj)[:, 0:GR]
 
     def largest(kind, at, beta_g, weight):
-        numer = sums[kind][:, 0:VH] - mm(proj, beta_g, HIGH)
+        numer = sums[kind] - mm(proj, beta_g, HIGH)
         pos = base + at
         inside = (pos >= first) & (pos < last)
         return jnp.max(jnp.where(inside, numer * numer * weight, 0.0), axis=1, keepdims=True)
@@ -471,8 +528,13 @@
             vmem((2, NZ, NG, NS), F32),
             vmem((TR, LO), F32),
             vmem((2, ROWS, NS), BF16),
-            vmem((2, ROWS, DW), F32),
-            vmem((2, 2, 4, CH, DW), F32),
+            vmem((2, ROWS, VH), F32),
+            vmem((NZ, 8, 128), F32),
+            vmem((NZ, 8, 128), F32),
+            vmem((2, 2, 2 * CH, HW), jnp.int16),
+            vmem((2, 2, 2, HW), F32),
+            vmem((2, 2, 4, 2 * CH, HW), jnp.int16),
+            vmem((2, 2, 4, 2, HW), F32),
             vmem((CH, 128), F32),
             vmem((CH, 128), F32),
             vmem((NZ, 8, 128), F32),
@@ -486,7 +548,8 @@
             dma((NZ,)), dma((NZ,)),
             dma, dma, dma, dma,
             dma((3,)), dma((3,)),
-            dma((2, 2, 4)), dma((2, 2, 4)),
+            dma((NZ,)), dma((NZ,)),
+            dma((2, 2, 2, 4)), dma((2, 2, 2, 4)),
             dma, dma,
             dma((NZ,)), dma((NZ,)),
         ],

time: 67.6 us -> 64.7 us (0.957)
  Pallas kernels: 64.3 us -> 61.4 us
    pallas_call x1, Pallas kernels: 64.3 us -> 61.4 us  [per_device(): pl.pallas_call(functools.partial(kernel, upto), out_shape=(jax.ShapeDtype...]
where the time goes in v3:
time: 64.7 us; the launch traced here: 64.5 us
  Pallas kernels  61.4 us (95%)
  local copies, waits for them, and re-layouts  2.48 us (4%)
    pallas_call x1, Pallas kernels, per_device(): pl.pallas_call(functools.partial(kernel, upto), out_shape=(jax.ShapeDtype...  61.4 us
    unnamed x2, local copies, waits for them, and re-layouts  2.48 us

profile of v3, /device:TPU:1, one launch (start us, length us, event | category | flops | bytes accessed | tf_op | source)
XLA Modules:
  0.0 64.5 jit_solution(16320782829528778673)
XLA Ops:
  0.6 61.4 %scan.1 = (f32[4,64]{1,0:T(4,128)}, f32[4,48]{1,0:T(4,128)}) custom-call(bf16[512,2048]{1,0:T(8,128)(2,1)} %geno.1, bf16[32,512]{1,0:T(8,128)(2,1)} %bitcast.3, f32[4,512]{1,0:T(4,128)} %bitcast.4, s32[48,512]{1,0:T(8,128)} %permh.1, s32[2,64]{1,0:T(2,128)} %bitcast.5), custom_call_target="tpu_custom_call" | custom-call | tf_op jit(solution)/shard_map/scan/pallas_call | solution.py:506
  62.1 1.2 %copy.9 = f32[4,64]{1,0:T(4,128)} copy(f32[4,64]{1,0:T(4,128)} %get-tuple-element.4) | data formatting | bytes 2048
  63.3 1.2 %copy.10 = f32[4,48]{1,0:T(4,128)} copy(f32[4,48]{1,0:T(4,128)} %get-tuple-element.5) | data formatting | bytes 1536

commit v4 on v3

--- a/solution.py
+++ b/solution.py
@@ -67,12 +67,12 @@
 def kernel(
     upto,
     geno, covh, pheh, permh, winh,
-    cur_ref, peak_ref,
+    out_ref,
     perm, win, xc, xy, xp, gs, gg, pk, gm, gcp, gr, ga, gh, yt, tab, yo, ds,
-    pq, pr, q0, s0, rb, sb, xs, xm, fm,
+    pq, pr, q0, s0, rb, sb, wm, fm,
     in_sem, geno_sem, g1_s, g1_r, p_s, p_r, pk_s, pk_r, c_s, c_r, f_s, f_r, h_s, h_r,
     gr_s, gr_r, ga_s, ga_r, gh_s, gh_r, t_s, t_r, y_s, y_r,
-    pr_s, pr_r, rs_s, rs_r, x_s, x_r, o_s, o_r,
+    pr_s, pr_r, rs_s, rs_r, o_s, o_r,
 ):
     s = lax.axis_index("samp")
     b = lax.axis_index("var")
@@ -121,8 +121,7 @@
         if upto != level:
             return False
         stop()
-        cur_ref[...] = jnp.zeros_like(cur_ref)
-        peak_ref[...] = jnp.zeros_like(peak_ref)
+        out_ref[...] = jnp.zeros_like(out_ref)
         return True
 
     other = dev(z, oc, b)
@@ -135,7 +134,7 @@
     for d in loads:
         d.start()
     barrier = pltpu.get_barrier_semaphore()
-    peers = [dev(zc(k), c, b) for k in range(1, NZ)] + [other]
+    peers = [dev(zc(k), cc, b) for k in range(1, NZ) for cc in (0, 1)] + [other]
     peers += [dev(z, cc, bb) for cc in (0, 1) for bb in (up_band, down_band)]
     for peer in peers:
         pl.semaphore_signal(barrier, inc=1, device_id=peer, device_id_type=MESH)
@@ -161,6 +160,12 @@
     pl.semaphore_wait(barrier, len(peers))
     start("g1", gg.at[c], gg.at[c], g1_s, g1_r, other, gg.at[oc], g1_r)
     start("p", xp.at[c], xp.at[c], p_s, p_r, other, xp.at[oc], p_r)
+
+    halo = gs.at[0, :, pl.ds(halo_at, VH)], gs.at[1, :, pl.ds(halo_at, VH)]
+    start("h0", geno.at[:, VH:2 * VH], gs.at[c, :, 0:VH], h_s.at[0], h_r.at[c],
+          dev(z, 0, up_band), halo[0], h_r.at[0])
+    start("h1", geno.at[:, 0:VH], gs.at[c, :, VH:2 * VH], h_s.at[1], h_r.at[c],
+          dev(z, 1, down_band), halo[1], h_r.at[1])
     if cut(0):
         own_geno.wait()
         return
@@ -192,12 +197,6 @@
     for to in (1, -1, 2, -2):
         share("c", 0, to)
         share("y", 0, to)
-    halo = gs.at[0, :, pl.ds(halo_at, VH)], gs.at[1, :, pl.ds(halo_at, VH)]
-    start("h0", geno.at[:, VH:2 * VH], gs.at[c, :, 0:VH], h_s.at[0], h_r.at[c],
-          dev(z, 0, up_band), halo[0], h_r.at[0])
-    start("h1", geno.at[:, 0:VH], gs.at[c, :, VH:2 * VH], h_s.at[1], h_r.at[c],
-          dev(z, 1, down_band), halo[1], h_r.at[1])
-
     own_geno.wait()
     landed("f")
     landed("p")
@@ -219,7 +218,7 @@
         dif = gs[lax.div(i, 32), at, pl.ds(own_at, VH)].astype(F32) - mean
         return acc + dif * dif
 
-    acc = lax.fori_loop(0, 64, spread, jnp.zeros((16, VH), F32))
+    acc = lax.fori_loop(0, 64, spread, jnp.zeros((16, VH), F32), unroll=4)
     rowg = iota((GR, VH), 0)
     gpart = jnp.where(rowg == GSP, jnp.sum(acc, axis=0, keepdims=True), gpart)
     for j in range(NZ):
@@ -379,6 +378,10 @@
             start((name, kind, way, t), here, land, rs_s.at[i, kind, way, t],
                   rs_r.at[i, kind, way, t], to, land, rs_r.at[i, kind, way, t])
 
+    product(0, own_at)
+    send_sum(0, 0, 0)
+    send_sum(0, 1, 0)
+
     proj = jnp.concatenate(
         [nt(yo[0], xp[0]) + nt(yo[1], xp[1]), jnp.zeros((ROWS, 128 - XR), F32)], axis=1
     )
@@ -391,17 +394,14 @@
             jnp.where(lane8 < 2 * GR, pltpu.roll(p3[1], GR, axis=1),
                       pltpu.roll(p3[2], 2 * GR, axis=1)),
         )
-    product(0, own_at)
-    send_sum(0, 0, 0)
-    send_sum(0, 1, 0)
+    for k in near:
+        start(("pr", k), pq.at[zc(k)], pr.at[z], pr_s.at[k], pr_r.at[NZ - k], dev(zc(k), c, b),
+              pr.at[zc(k)], pr_r.at[k])
     landed("h0")
     landed("h1")
     product(1, halo_at)
     send_sum(1, 1, 0)
     send_sum(1, 0, 0)
-    for k in near:
-        start(("pr", k), pq.at[zc(k)], pr.at[z], pr_s.at[k], pr_r.at[NZ - k], dev(zc(k), c, b),
-              pr.at[zc(k)], pr_r.at[k])
     if cut(5):
         return
 
@@ -424,10 +424,8 @@
         send_sum(kind, way, 1)
     landed("gh")
     beta_halo, weight_halo = of_variants(gh)
-    for t in range(2, 4):
-        for kind, way in order:
-            if t < hops(kind, way):
-                send_sum(kind, way, t)
+    for kind, way in order:
+        send_sum(kind, way, 2)
 
     gene24 = lax.rem(iota((CH, 1), 0), NG)
     first = jnp.zeros((CH, 1), jnp.int32)
@@ -449,68 +447,70 @@
     l24 = iota((CH, 128), 1)
     proj = jnp.where((l24 < NC) | (l24 == GONE), proj, 0.0)[:, 0:GR]
 
-    sums = []
+    for kind, (at, beta_g, weight) in enumerate(
+        ((own_at, beta_own, weight_own), (halo_at, beta_halo, weight_halo))
+    ):
+        lines = pl.ds(pl.multiple_of(z * CH, CH), CH)
+        ds[kind, lines, :] = ds[kind, lines, :] - mm(proj, beta_g, HIGH)
+        pos = base + at
+        wm[kind] = jnp.where((pos >= first) & (pos < last), weight, 0.0)
+    for kind, way in order:
+        if hops(kind, way) > 3:
+            send_sum(kind, way, 3)
+
+    best = jnp.zeros((CH, HW), F32)
     for kind in range(2):
         parts = halves(chunk(kind, 0))
-        for way in range(2):
+        for way in (0, 1) if hops(kind, 1) > 3 else (1, 0):
             end = hops(kind, way) - 1
             landed(("rs", kind, way, end))
             landed(("sc", kind, way, end))
             got = unpack(rb.at[kind, way, end], sb.at[kind, way, end])
             parts = [u + v for u, v in zip(parts, got)]
-        sums.append(jnp.concatenate(parts, axis=1))
+        for h in range(2):
+            best = jnp.maximum(best, parts[h] * parts[h] * wm[kind, :, HW * h:HW * (h + 1)])
     if cut(6):
         return
-
-    def largest(kind, at, beta_g, weight):
-        numer = sums[kind] - mm(proj, beta_g, HIGH)
-        pos = base + at
-        inside = (pos >= first) & (pos < last)
-        return jnp.max(jnp.where(inside, numer * numer * weight, 0.0), axis=1, keepdims=True)
-
-    best = jnp.maximum(
-        largest(0, own_at, beta_own, weight_own), largest(1, halo_at, beta_halo, weight_halo)
-    )
-    xs[...] = jnp.broadcast_to(best, (CH, 128))
-    start("x", xs, xm, x_s, x_r, other, xm, x_r)
-    landed("x")
-    best = jnp.maximum(xs[...], xm[...]) * float(NSAMP)
+    best = jnp.max(best, axis=1, keepdims=True) * float(NSAMP)
 
     r24, l24 = iota((CH, 128), 0), iota((CH, 128), 1)
     placed = jnp.where(l24 == lax.shift_right_logical(r24, 2) + PZ * z, best, 0.0)
-    level = LEVMAX * l24.astype(F32) / (LEVELS - 1)
-    curve = jax.nn.sigmoid(best - level)
-
-    def over_perms(v):
-        v = (v[0:8] + v[8:16]) + v[16:24]
-        return v + pltpu.roll(v, NG, axis=0)
-
-    fm[z] = jnp.where(iota((8, 128), 0) < NG, over_perms(placed), over_perms(curve))
-    for k in near:
-        start(("o", k), fm.at[z], fm.at[z], o_s.at[k], o_r.at[NZ - k], dev(zc(k), c, b),
-              fm.at[zc(k)], o_r.at[k])
-    for k in range(1, NZ):
-        landed(("o", k))
-    both = fm[0]
+    placed = (placed[0:8] + placed[8:16]) + placed[16:24]
+    fm[c, z] = placed + pltpu.roll(placed, NG, axis=0)
+    for cc in range(2):
+        to = lax.rem(c + cc, 2)
+        for k in near + ((0,) if cc else ()):
+            start(("o", cc, k), fm.at[c, z], fm.at[c, z], o_s.at[cc, k],
+                  o_r.at[cc, (NZ - k) % NZ], dev(zc(k), to, b), fm.at[to, zc(k)], o_r.at[cc, k])
+    for key in [("o", 1, 0)] + [("o", cc, k) for k in near for cc in range(2)]:
+        landed(key)
+    both = [fm[cc, 0] for cc in range(2)]
     for j in range(1, NZ):
-        both = both + fm[j]
-    peak_ref[...] = both[0:NG, 0:NP]
-    cur_ref[...] = both[NG:2 * NG, 0:LEVELS] * (1.0 / NP)
+        both = [v + fm[cc, j] for cc, v in enumerate(both)]
+    peak = jnp.maximum(both[0], both[1])
+    columns = peak.T
+    level = LEVMAX * iota((NP, 128), 1).astype(F32) / (LEVELS - 1)
+    out_ref[0:NG, :] = peak[0:NG]
+    for g in range(NG):
+        curve = jax.nn.sigmoid(columns[0:NP, g:g + 1] - level)
+        out_ref[NG + g:NG + g + 1, :] = jnp.sum(curve, axis=0, keepdims=True) * (1.0 / NP)
     stop()
+
+
+def split(both_ref, cur_ref, peak_ref):
+    peak_ref[...] = both_ref[0:NG, 0:NP]
+    cur_ref[...] = both_ref[NG:2 * NG, 0:LEVELS]
 
 
 def per_device(upto, geno, covar, pheno, perm, windows):
     dma = pltpu.SemaphoreType.DMA
     vmem = pltpu.VMEM
     spec = pl.BlockSpec(memory_space=pltpu.VMEM)
-    return pl.pallas_call(
+    both = pl.pallas_call(
         functools.partial(kernel, upto),
-        out_shape=(
-            jax.ShapeDtypeStruct((NG, LEVELS), F32),
-            jax.ShapeDtypeStruct((NG, NP), F32),
-        ),
+        out_shape=jax.ShapeDtypeStruct((2 * NG, 128), F32),
         in_specs=[pl.BlockSpec(memory_space=pltpu.HBM)] * 5,
-        out_specs=(spec, spec),
+        out_specs=spec,
         scratch_shapes=[
             vmem((NP, NS), jnp.int32),
             pltpu.SMEM((2, NG * NB), jnp.int32),
@@ -535,9 +535,8 @@
             vmem((2, 2, 2, HW), F32),
             vmem((2, 2, 4, 2 * CH, HW), jnp.int16),
             vmem((2, 2, 4, 2, HW), F32),
-            vmem((CH, 128), F32),
-            vmem((CH, 128), F32),
-            vmem((NZ, 8, 128), F32),
+            vmem((2, CH, VH), F32),
+            vmem((2, NZ, 8, 128), F32),
             dma((4,)), dma,
             dma, dma, dma, dma,
             dma((NZ,)), dma((NZ,)),
@@ -550,14 +549,23 @@
             dma((3,)), dma((3,)),
             dma((NZ,)), dma((NZ,)),
             dma((2, 2, 2, 4)), dma((2, 2, 2, 4)),
-            dma, dma,
-            dma((NZ,)), dma((NZ,)),
+            dma((2, NZ)), dma((2, NZ)),
         ],
         compiler_params=pltpu.CompilerParams(
             collective_id=0, has_side_effects=True, vmem_limit_bytes=56 * 1024 * 1024
         ),
         name="scan",
     )(geno, covar.T, pheno.T, perm, windows.T)
+    return pl.pallas_call(
+        split,
+        out_shape=(
+            jax.ShapeDtypeStruct((NG, LEVELS), F32),
+            jax.ShapeDtypeStruct((NG, NP), F32),
+        ),
+        in_specs=[spec],
+        out_specs=(spec, spec),
+        name="split",
+    )(both)
 
 
 def build(mesh, upto):

time: 64.7 us -> 62.4 us (0.964)
  local copies, waits for them, and re-layouts: 2.48 us -> 0 us
    unnamed x2 -> x0, local copies, waits for them, and re-layouts: 2.48 us -> none
    pallas_call x1 -> x2, Pallas kernels: 61.4 us -> 61.7 us  [the longest x1 60.4 us: per_device(): pl.pallas_call(functools.partial(kernel, upto), out_shape=jax.ShapeDtypeS...]
where the time goes in v4:
time: 62.4 us; the launch traced here: 62.3 us
  Pallas kernels  61.7 us (99%)
  between operations  0.64 us (1%)
    pallas_call x1, Pallas kernels, per_device(): pl.pallas_call(functools.partial(kernel, upto), out_shape=jax.ShapeDtypeS...  60.4 us
    pallas_call x1, Pallas kernels, per_device(): pl.pallas_call(split, out_shape=(jax.ShapeDtypeStruct((NG, LEVELS), F32),...  1.27 us

profile of v4, /device:TPU:1, one launch (start us, length us, event | category | flops | bytes accessed | tf_op | source)
XLA Modules:
  0.0 62.3 jit_solution(11636961961161787270)
XLA Ops:
  0.6 60.4 %scan.1.both_ref = f32[8,128]{1,0:T(8,128)} custom-call(bf16[512,2048]{1,0:T(8,128)(2,1)} %geno.1, bf16[32,512]{1,0:T(8,128)(2,1)} %bitcast.3, f32[4,512]{1,0:T(4,128)} %bitcast.4, s32[48,512]{1,0:T(8,128)} %permh.1, s32[2,64]{1,0:T(2,128)} %bitcast.5), custom_call_target="tpu_custom_call" | custom-call | tf_op jit(solution)/shard_map/scan/pallas_call | solution.py:509
  61.0 1.3 %split.1 = (f32[4,64]{1,0:T(4,128)}, f32[4,48]{1,0:T(4,128)}) custom-call(f32[8,128]{1,0:T(8,128)} %scan.1.both_ref), custom_call_target="tpu_custom_call" | custom-call | tf_op jit(solution)/shard_map/split/pallas_call | solution.py:559

commit v5 on v4

--- a/solution.py
+++ b/solution.py
@@ -10,6 +10,7 @@
 MESH = pl.DeviceIdType.MESH
 F32 = jnp.float32
 BF16 = jnp.bfloat16
+I16 = jnp.int16
 HIGH = lax.Precision.HIGHEST
 
 EPS = 1e-06
@@ -33,7 +34,9 @@
 GSP = 37
 ROWS = NG * NP
 CH = ROWS // NZ
-HW = VH // 2
+WA = 768
+WB = VH - WA
+WIDTHS = (VH, WA, WB)
 QMAX = 32767.0
 TINY = 1e-30
 HOPS = (4, 3)
@@ -69,10 +72,10 @@
     geno, covh, pheh, permh, winh,
     out_ref,
     perm, win, xc, xy, xp, gs, gg, pk, gm, gcp, gr, ga, gh, yt, tab, yo, ds,
-    pq, pr, q0, s0, rb, sb, wm, fm,
+    pq, pr, q0, s0, rb, sb, qd, sd, rd, td, wm, fm,
     in_sem, geno_sem, g1_s, g1_r, p_s, p_r, pk_s, pk_r, c_s, c_r, f_s, f_r, h_s, h_r,
     gr_s, gr_r, ga_s, ga_r, gh_s, gh_r, t_s, t_r, y_s, y_r,
-    pr_s, pr_r, rs_s, rs_r, o_s, o_r,
+    pr_s, pr_r, rs_s, rs_r, d_s, d_r, o_s, o_r,
 ):
     s = lax.axis_index("samp")
     b = lax.axis_index("var")
@@ -161,11 +164,17 @@
     start("g1", gg.at[c], gg.at[c], g1_s, g1_r, other, gg.at[oc], g1_r)
     start("p", xp.at[c], xp.at[c], p_s, p_r, other, xp.at[oc], p_r)
 
-    halo = gs.at[0, :, pl.ds(halo_at, VH)], gs.at[1, :, pl.ds(halo_at, VH)]
-    start("h0", geno.at[:, VH:2 * VH], gs.at[c, :, 0:VH], h_s.at[0], h_r.at[c],
-          dev(z, 0, up_band), halo[0], h_r.at[0])
-    start("h1", geno.at[:, 0:VH], gs.at[c, :, VH:2 * VH], h_s.at[1], h_r.at[c],
-          dev(z, 1, down_band), halo[1], h_r.at[1])
+    def send_halo(piece):
+        skip, width = ((0, WA), (WA, WB))[piece]
+        for i, (cc, band) in enumerate(((0, up_band), (1, down_band))):
+            start(
+                ("h", piece, i), geno.at[:, pl.ds((1 - cc) * VH + skip, width)],
+                gs.at[c, :, pl.ds(cc * VH + skip, width)], h_s.at[piece, i], h_r.at[piece, c],
+                dev(z, cc, band),
+                gs.at[i, :, pl.ds(pl.multiple_of(halo_at + skip, 128), width)], h_r.at[piece, i],
+            )
+
+    send_halo(0)
     if cut(0):
         own_geno.wait()
         return
@@ -269,6 +278,7 @@
         fit = (t[16:24] + t[8:16]) + t[0:8]
         yt[c, zc(k)] = xy[zc(k)] - (fit[0:4] + const)
     start("t", yt.at[c], yt.at[c], t_s, t_r, other, yt.at[oc], t_r)
+    send_halo(1)
 
     landed("t")
     ysq = jnp.zeros((NG, NS), F32)
@@ -339,10 +349,11 @@
         landed(("yo", j))
 
     def product(kind, at):
-        ds[kind] = mm(yo[0], gs[0, :, pl.ds(at, VH)]) + mm(yo[1], gs[1, :, pl.ds(at, VH)])
+        lanes = pl.ds(pl.multiple_of(at, 128), WIDTHS[kind])
+        ds[kind][...] = mm(yo[0], gs[0, :, lanes]) + mm(yo[1], gs[1, :, lanes])
 
     def chunk(kind, k):
-        return ds.at[kind, pl.ds(pl.multiple_of(zc(k) * CH, CH), CH)]
+        return ds[kind].at[pl.ds(pl.multiple_of(zc(k) * CH, CH), CH)]
 
     def hops(kind, way):
         return HOPS[(kind + way) % 2]
@@ -352,29 +363,33 @@
         return [q[CH * h:CH * (h + 1)] * scale[h:h + 1, :] for h in range(2)]
 
     def halves(ref):
-        return [ref[:, HW * h:HW * (h + 1)] for h in range(2)]
-
-    def send_sum(kind, way, t):
-        n = hops(kind, way)
-        sign = 1 - 2 * way
-        parts = halves(chunk(kind, -sign * (n - t)))
-        if t == 0:
-            src, scale = q0.at[kind, way], s0.at[kind, way]
-        else:
-            src, scale = rb.at[kind, way, t - 1], sb.at[kind, way, t - 1]
-            landed(("rs", kind, way, t - 1))
-            landed(("sc", kind, way, t - 1))
-            parts = [u + v for u, v in zip(parts, unpack(src, scale))]
+        w = ref.shape[1] // 2
+        return [ref[:, w * h:w * (h + 1)] for h in range(2)]
+
+    def pack(parts, ref, scale):
         codes = []
         for h in range(2):
             top = jnp.max(jnp.abs(parts[h]), axis=0, keepdims=True)
             top = jnp.maximum(top, TINY)
             scale[h:h + 1, :] = top * (1.0 / QMAX)
             codes.append(jnp.round(parts[h] * (QMAX / top)))
-        src[...] = jnp.concatenate(codes, axis=0).astype(jnp.int32).astype(jnp.int16)
+        ref[...] = jnp.concatenate(codes, axis=0).astype(jnp.int32).astype(jnp.int16)
+
+    def send_sum(kind, way, t):
+        n = hops(kind, way)
+        sign = 1 - 2 * way
+        parts = halves(chunk(kind, -sign * (n - t)))
+        if t == 0:
+            src, scale = q0[kind].at[way], s0[kind].at[way]
+        else:
+            src, scale = rb[kind].at[way, t - 1], sb[kind].at[way, t - 1]
+            landed(("rs", kind, way, t - 1))
+            landed(("sc", kind, way, t - 1))
+            parts = [u + v for u, v in zip(parts, unpack(src, scale))]
+        pack(parts, src, scale)
         to = dev(zc(-sign), c, b)
         for i, (name, here, buf) in enumerate((("rs", src, rb), ("sc", scale, sb))):
-            land = buf.at[kind, way, t]
+            land = buf[kind].at[way, t]
             start((name, kind, way, t), here, land, rs_s.at[i, kind, way, t],
                   rs_r.at[i, kind, way, t], to, land, rs_r.at[i, kind, way, t])
 
@@ -397,8 +412,8 @@
     for k in near:
         start(("pr", k), pq.at[zc(k)], pr.at[z], pr_s.at[k], pr_r.at[NZ - k], dev(zc(k), c, b),
               pr.at[zc(k)], pr_r.at[k])
-    landed("h0")
-    landed("h1")
+    landed(("h", 0, 0))
+    landed(("h", 0, 1))
     product(1, halo_at)
     send_sum(1, 1, 0)
     send_sum(1, 0, 0)
@@ -422,6 +437,15 @@
     order = ((0, 0), (0, 1), (1, 1), (1, 0))
     for kind, way in order:
         send_sum(kind, way, 1)
+
+    landed(("h", 1, 0))
+    landed(("h", 1, 1))
+    product(2, halo_at + WA)
+    for k in near:
+        pack(halves(chunk(2, k)), qd.at[zc(k)], sd.at[zc(k)])
+        for i, (name, here, there) in enumerate((("dr", qd, rd), ("dc", sd, td))):
+            start((name, k), here.at[zc(k)], there.at[z], d_s.at[i, k], d_r.at[i, NZ - k],
+                  dev(zc(k), c, b), there.at[zc(k)], d_r.at[i, k])
     landed("gh")
     beta_halo, weight_halo = of_variants(gh)
     for kind, way in order:
@@ -447,28 +471,42 @@
     l24 = iota((CH, 128), 1)
     proj = jnp.where((l24 < NC) | (l24 == GONE), proj, 0.0)[:, 0:GR]
 
-    for kind, (at, beta_g, weight) in enumerate(
-        ((own_at, beta_own, weight_own), (halo_at, beta_halo, weight_halo))
-    ):
-        lines = pl.ds(pl.multiple_of(z * CH, CH), CH)
-        ds[kind, lines, :] = ds[kind, lines, :] - mm(proj, beta_g, HIGH)
-        pos = base + at
-        wm[kind] = jnp.where((pos >= first) & (pos < last), weight, 0.0)
+    fits = (
+        (own_at, beta_own, weight_own),
+        (halo_at, beta_halo[:, 0:WA], weight_halo[:, 0:WA]),
+        (halo_at + WA, beta_halo[:, WA:VH], weight_halo[:, WA:VH]),
+    )
+    lines = pl.ds(pl.multiple_of(z * CH, CH), CH)
+    for kind, (at, beta_g, weight) in enumerate(fits):
+        ds[kind][lines, :] = ds[kind][lines, :] - mm(proj, beta_g, HIGH)
+        pos = base[:, 0:WIDTHS[kind]] + at
+        wm[kind][...] = jnp.where((pos >= first) & (pos < last), weight, 0.0)
     for kind, way in order:
         if hops(kind, way) > 3:
             send_sum(kind, way, 3)
 
-    best = jnp.zeros((CH, HW), F32)
+    def squares(kind, parts):
+        v = jnp.concatenate(parts, axis=1)
+        v = v * v * wm[kind][...]
+        return functools.reduce(
+            jnp.maximum, [v[:, i:i + 128] for i in range(0, WIDTHS[kind], 128)]
+        )
+
+    parts = halves(chunk(2, 0))
+    for k in near:
+        landed(("dr", k))
+        landed(("dc", k))
+        parts = [u + v for u, v in zip(parts, unpack(rd.at[zc(k)], td.at[zc(k)]))]
+    best = squares(2, parts)
     for kind in range(2):
         parts = halves(chunk(kind, 0))
         for way in (0, 1) if hops(kind, 1) > 3 else (1, 0):
             end = hops(kind, way) - 1
             landed(("rs", kind, way, end))
             landed(("sc", kind, way, end))
-            got = unpack(rb.at[kind, way, end], sb.at[kind, way, end])
+            got = unpack(rb[kind].at[way, end], sb[kind].at[way, end])
             parts = [u + v for u, v in zip(parts, got)]
-        for h in range(2):
-            best = jnp.maximum(best, parts[h] * parts[h] * wm[kind, :, HW * h:HW * (h + 1)])
+        best = jnp.maximum(best, squares(kind, parts))
     if cut(6):
         return
     best = jnp.max(best, axis=1, keepdims=True) * float(NSAMP)
@@ -476,7 +514,7 @@
     r24, l24 = iota((CH, 128), 0), iota((CH, 128), 1)
     placed = jnp.where(l24 == lax.shift_right_logical(r24, 2) + PZ * z, best, 0.0)
     placed = (placed[0:8] + placed[8:16]) + placed[16:24]
-    fm[c, z] = placed + pltpu.roll(placed, NG, axis=0)
+    fm[c, z] = (placed + pltpu.roll(placed, NG, axis=0))[0:NG]
     for cc in range(2):
         to = lax.rem(c + cc, 2)
         for k in near + ((0,) if cc else ()):
@@ -488,9 +526,9 @@
     for j in range(1, NZ):
         both = [v + fm[cc, j] for cc, v in enumerate(both)]
     peak = jnp.maximum(both[0], both[1])
-    columns = peak.T
+    columns = jnp.concatenate([peak, peak], axis=0).T
     level = LEVMAX * iota((NP, 128), 1).astype(F32) / (LEVELS - 1)
-    out_ref[0:NG, :] = peak[0:NG]
+    out_ref[0:NG, :] = peak
     for g in range(NG):
         curve = jax.nn.sigmoid(columns[0:NP, g:g + 1] - level)
         out_ref[NG + g:NG + g + 1, :] = jnp.sum(curve, axis=0, keepdims=True) * (1.0 / NP)
@@ -528,27 +566,32 @@
             vmem((2, NZ, NG, NS), F32),
             vmem((TR, LO), F32),
             vmem((2, ROWS, NS), BF16),
-            vmem((2, ROWS, VH), F32),
+            [vmem((ROWS, w), F32) for w in WIDTHS],
             vmem((NZ, 8, 128), F32),
             vmem((NZ, 8, 128), F32),
-            vmem((2, 2, 2 * CH, HW), jnp.int16),
-            vmem((2, 2, 2, HW), F32),
-            vmem((2, 2, 4, 2 * CH, HW), jnp.int16),
-            vmem((2, 2, 4, 2, HW), F32),
-            vmem((2, CH, VH), F32),
-            vmem((2, NZ, 8, 128), F32),
+            [vmem((2, 2 * CH, w // 2), I16) for w in WIDTHS[:2]],
+            [vmem((2, 2, w // 2), F32) for w in WIDTHS[:2]],
+            [vmem((2, 4, 2 * CH, w // 2), I16) for w in WIDTHS[:2]],
+            [vmem((2, 4, 2, w // 2), F32) for w in WIDTHS[:2]],
+            vmem((NZ, 2 * CH, WB // 2), I16),
+            vmem((NZ, 2, WB // 2), F32),
+            vmem((NZ, 2 * CH, WB // 2), I16),
+            vmem((NZ, 2, WB // 2), F32),
+            [vmem((CH, w), F32) for w in WIDTHS],
+            vmem((2, NZ, NG, 128), F32),
             dma((4,)), dma,
             dma, dma, dma, dma,
             dma((NZ,)), dma((NZ,)),
             dma((2, NZ)), dma((2, NZ)),
             dma, dma,
-            dma((2,)), dma((2,)),
+            dma((2, 2)), dma((2, 2)),
             dma((NZ,)), dma((NZ,)),
             dma((NZ,)), dma((NZ,)),
             dma, dma, dma, dma,
             dma((3,)), dma((3,)),
             dma((NZ,)), dma((NZ,)),
             dma((2, 2, 2, 4)), dma((2, 2, 2, 4)),
+            dma((2, NZ)), dma((2, NZ)),
             dma((2, NZ)), dma((2, NZ)),
         ],
         compiler_params=pltpu.CompilerParams(

time: 62.4 us -> 57.5 us (0.921)
  Pallas kernels: 61.7 us -> 56.7 us
    pallas_call x1, Pallas kernels: 60.4 us -> 55.5 us  [per_device(): pl.pallas_call(functools.partial(kernel, upto), out_shape=jax.ShapeDtypeS...]
where the time goes in v5:
time: 57.5 us; the launch traced here: 57.4 us
  Pallas kernels  56.7 us (99%)
  between operations  0.64 us (1%)
    pallas_call x1, Pallas kernels, per_device(): pl.pallas_call(functools.partial(kernel, upto), out_shape=jax.ShapeDtypeS...  55.5 us
    pallas_call x1, Pallas kernels, per_device(): pl.pallas_call(split, out_shape=(jax.ShapeDtypeStruct((NG, LEVELS), F32),...  1.27 us

profile of v5, /device:TPU:1, one launch (start us, length us, event | category | flops | bytes accessed | tf_op | source)
XLA Modules:
  0.0 57.4 jit_solution(7007482935798634875)
XLA Ops:
  0.6 55.5 %scan.1.both_ref = f32[8,128]{1,0:T(8,128)} custom-call(bf16[512,2048]{1,0:T(8,128)(2,1)} %geno.1, bf16[32,512]{1,0:T(8,128)(2,1)} %bitcast.3, f32[4,512]{1,0:T(4,128)} %bitcast.4, s32[48,512]{1,0:T(8,128)} %permh.1, s32[2,64]{1,0:T(2,128)} %bitcast.5), custom_call_target="tpu_custom_call" | custom-call | tf_op jit(solution)/shard_map/scan/pallas_call | solution.py:547
  56.1 1.3 %split.1 = (f32[4,64]{1,0:T(4,128)}, f32[4,48]{1,0:T(4,128)}) custom-call(f32[8,128]{1,0:T(8,128)} %scan.1.both_ref), custom_call_target="tpu_custom_call" | custom-call | tf_op jit(solution)/shard_map/split/pallas_call | solution.py:602

commit v6 on v5

--- a/solution.py
+++ b/solution.py
@@ -162,8 +162,6 @@
 
     pl.semaphore_wait(barrier, len(peers))
     start("g1", gg.at[c], gg.at[c], g1_s, g1_r, other, gg.at[oc], g1_r)
-    start("p", xp.at[c], xp.at[c], p_s, p_r, other, xp.at[oc], p_r)
-
     def send_halo(piece):
         skip, width = ((0, WA), (WA, WB))[piece]
         for i, (cc, band) in enumerate(((0, up_band), (1, down_band))):
@@ -173,8 +171,18 @@
                 dev(z, cc, band),
                 gs.at[i, :, pl.ds(pl.multiple_of(halo_at + skip, 128), width)], h_r.at[piece, i],
             )
-
     send_halo(0)
+
+    def share(name, held, to):
+        ref = (xc, xy)[name == "y"]
+        i, k, got = int(name == "y"), (held - to) % NZ, zc(held - to)
+        start((name, k), ref.at[zc(held)], ref.at[zc(held)], c_s.at[i, k], c_r.at[i, k],
+              dev(zc(to), c, b), ref.at[got], c_r.at[i, k])
+
+    for to in (1, -1, 2, -2):
+        share("c", 0, to)
+        share("y", 0, to)
+    start("p", xp.at[c], xp.at[c], p_s, p_r, other, xp.at[oc], p_r)
     if cut(0):
         own_geno.wait()
         return
@@ -197,21 +205,6 @@
     start("f", geno.at[:, half(oc)], gs.at[c, :, half(c)], f_s, f_r, other,
           gs.at[oc, :, pl.ds(own_at, VH)], f_r)
 
-    def share(name, held, to):
-        ref = (xc, xy)[name == "y"]
-        i, k, got = int(name == "y"), (held - to) % NZ, zc(held - to)
-        start((name, k), ref.at[zc(held)], ref.at[zc(held)], c_s.at[i, k], c_r.at[i, k],
-              dev(zc(to), c, b), ref.at[got], c_r.at[i, k])
-
-    for to in (1, -1, 2, -2):
-        share("c", 0, to)
-        share("y", 0, to)
-    own_geno.wait()
-    landed("f")
-    landed("p")
-    gpart = fold_rows(
-        mm(xp[0], gs[0, :, pl.ds(own_at, VH)]) + mm(xp[1], gs[1, :, pl.ds(own_at, VH)])
-    )
     for name in ("c", "y"):
         for k in (6, 2):
             landed((name, k))
@@ -220,6 +213,13 @@
     for name in ("c", "y"):
         share(name, -2, 1)
         share(name, 2, -1)
+
+    own_geno.wait()
+    landed("f")
+    landed("p")
+    gpart = fold_rows(
+        mm(xp[0], gs[0, :, pl.ds(own_at, VH)]) + mm(xp[1], gs[1, :, pl.ds(own_at, VH)])
+    )
     mean = gpart[GONE:GONE + 1, :] * (1.0 / (2 * NS))
 
     def spread(i, acc):
@@ -251,15 +251,24 @@
     in_lane = (lane < NC) | (lane == GONE)
     a = jnp.where(in_lane, a, 0.0)
     colmean = a[:, GONE:GONE + 1] * (1.0 / NSAMP)
-    for k in (GONE,) + tuple(range(NC)):
-        q = a[:, k:k + 1]
-        r = a[k:k + 1, :]
-        inv = 1.0 / a[k:k + 1, k:k + 1]
-        rr = r * inv
-        nxt = a - q * rr
-        nxt = jnp.where(row == k, rr, nxt)
-        nxt = jnp.where(lane == k, jnp.where(row == k, -inv, q * inv), nxt)
-        a = nxt
+    r = a[GONE:GONE + 1, :]
+    inv = 1.0 / a[GONE:GONE + 1, GONE:GONE + 1]
+    q = a[:, GONE:GONE + 1]
+    nxt = jnp.where(row == GONE, r * inv, a - q * (r * inv))
+    a = jnp.where(lane == GONE, jnp.where(row == GONE, -inv, q * inv), nxt)
+    for k in range(0, NC, 2):
+        m = k + 1
+        q1, q2 = a[:, k:k + 1], a[:, m:m + 1]
+        r1, r2 = a[k:k + 1, :], a[m:m + 1, :]
+        p, o, w = a[k:k + 1, k:k + 1], a[k:k + 1, m:m + 1], a[m:m + 1, m:m + 1]
+        det = 1.0 / (p * w - o * o)
+        p, o, w = p * det, o * det, w * det
+        t1, t2 = w * r1 - o * r2, p * r2 - o * r1
+        nxt = a - q1 * t1 - q2 * t2
+        nxt = jnp.where(row == k, t1, jnp.where(row == m, t2, nxt))
+        c1 = jnp.where(row == k, -w, jnp.where(row == m, o, w * q1 - o * q2))
+        c2 = jnp.where(row == k, o, jnp.where(row == m, -p, p * q2 - o * q1))
+        a = jnp.where(lane == k, c1, jnp.where(lane == m, c2, nxt))
     gm[...] = jnp.where(in_row & in_lane, -a, 0.0)
 
     beta = a[32:40, :]
@@ -278,7 +287,6 @@
         fit = (t[16:24] + t[8:16]) + t[0:8]
         yt[c, zc(k)] = xy[zc(k)] - (fit[0:4] + const)
     start("t", yt.at[c], yt.at[c], t_s, t_r, other, yt.at[oc], t_r)
-    send_halo(1)
 
     landed("t")
     ysq = jnp.zeros((NG, NS), F32)
@@ -331,7 +339,12 @@
         for j in range(NZ):
             off = gr[j, GONE:GONE + 1, :] * (1.0 / (2 * NS)) - mu
             between = between + off * off
-        ga[z] = tot + jnp.where(row == GSP, between * (2.0 * NS), 0.0)
+        centred = jnp.where(row < NC, tot - colmean * tot[GONE:GONE + 1, :], 0.0)
+        slope = mm(gm[:, 0:GR], centred, HIGH)
+        explained = jnp.sum(centred * slope, axis=0, keepdims=True)
+        spread_all = tot[GSP:GSP + 1, :] + between * (2.0 * NS)
+        weight = 1.0 / (jnp.maximum(spread_all - explained, 0.0) + EPS)
+        ga[z] = jnp.where(row == GSP, weight, jnp.where(row == GONE, slope + mu, slope))
         for k in near:
             start(("ga", k), ga.at[z], ga.at[z], ga_s.at[k], ga_r.at[NZ - k], dev(zc(k), c, b),
                   ga.at[zc(k)], ga_r.at[k])
@@ -342,6 +355,7 @@
         start(("yo", j), yo.at[c, part], yo.at[c, part], y_s.at[j], y_r.at[j], other,
               yo.at[oc, part], y_r.at[j])
         if j == 0:
+            send_halo(1)
             sum_variants()
     if cut(4):
         return
@@ -420,20 +434,6 @@
     if cut(5):
         return
 
-    for k in range(1, NZ):
-        landed(("ga", k))
-    start("gh", ga, gh, gh_s, gh_r, dev(z, oc, nbr), gh, gh_r)
-
-    inv = gm[:, 0:GR]
-
-    def of_variants(ref):
-        gx = jnp.concatenate([ref[j] for j in range(NZ)], axis=1)
-        centred = jnp.where(rowg < NC, gx - colmean * gx[GONE:GONE + 1, :], 0.0)
-        explained = jnp.sum(centred * mm(inv, centred, HIGH), axis=0, keepdims=True)
-        weight = 1.0 / (jnp.maximum(gx[GSP:GSP + 1, :] - explained, 0.0) + EPS)
-        return mm(inv, jnp.where((rowg < NC) | (rowg == GONE), gx, 0.0), HIGH), weight
-
-    beta_own, weight_own = of_variants(ga)
     order = ((0, 0), (0, 1), (1, 1), (1, 0))
     for kind, way in order:
         send_sum(kind, way, 1)
@@ -446,8 +446,10 @@
         for i, (name, here, there) in enumerate((("dr", qd, rd), ("dc", sd, td))):
             start((name, k), here.at[zc(k)], there.at[z], d_s.at[i, k], d_r.at[i, NZ - k],
                   dev(zc(k), c, b), there.at[zc(k)], d_r.at[i, k])
-    landed("gh")
-    beta_halo, weight_halo = of_variants(gh)
+    for k in range(1, NZ):
+        landed(("ga", k))
+    start("gh", ga, gh, gh_s, gh_r, dev(z, oc, nbr), gh, gh_r)
+
     for kind, way in order:
         send_sum(kind, way, 2)
 
@@ -471,19 +473,23 @@
     l24 = iota((CH, 128), 1)
     proj = jnp.where((l24 < NC) | (l24 == GONE), proj, 0.0)[:, 0:GR]
 
-    fits = (
-        (own_at, beta_own, weight_own),
-        (halo_at, beta_halo[:, 0:WA], weight_halo[:, 0:WA]),
-        (halo_at + WA, beta_halo[:, WA:VH], weight_halo[:, WA:VH]),
-    )
-    lines = pl.ds(pl.multiple_of(z * CH, CH), CH)
-    for kind, (at, beta_g, weight) in enumerate(fits):
-        ds[kind][lines, :] = ds[kind][lines, :] - mm(proj, beta_g, HIGH)
-        pos = base[:, 0:WIDTHS[kind]] + at
-        wm[kind][...] = jnp.where((pos >= first) & (pos < last), weight, 0.0)
     for kind, way in order:
         if hops(kind, way) > 3:
             send_sum(kind, way, 3)
+
+    def fit(ref, kinds):
+        both = jnp.concatenate([ref[j] for j in range(NZ)], axis=1)
+        lines = pl.ds(pl.multiple_of(z * CH, CH), CH)
+        for kind, at, skip in kinds:
+            beta_g = both[:, skip:skip + WIDTHS[kind]]
+            ds[kind][lines, :] = ds[kind][lines, :] - mm(proj, beta_g, HIGH)
+            pos = base[:, 0:WIDTHS[kind]] + at
+            inside = (pos >= first) & (pos < last)
+            wm[kind][...] = jnp.where(inside, beta_g[GSP:GSP + 1, :], 0.0)
+
+    fit(ga, ((0, own_at, 0),))
+    landed("gh")
+    fit(gh, ((1, halo_at, 0), (2, halo_at + WA, WA)))
 
     def squares(kind, parts):
         v = jnp.concatenate(parts, axis=1)

time: 57.5 us -> 56.8 us (0.988)
  Pallas kernels: 56.7 us -> 56.1 us
    pallas_call x1, Pallas kernels: 55.5 us -> 54.8 us  [per_device(): pl.pallas_call(functools.partial(kernel, upto), out_shape=jax.ShapeDtypeS...]
where the time goes in v6:
time: 56.8 us; the launch traced here: 56.7 us
  Pallas kernels  56.1 us (99%)
  between operations  0.64 us (1%)
    pallas_call x1, Pallas kernels, per_device(): pl.pallas_call(functools.partial(kernel, upto), out_shape=jax.ShapeDtypeS...  54.8 us
    pallas_call x1, Pallas kernels, per_device(): pl.pallas_call(split, out_shape=(jax.ShapeDtypeStruct((NG, LEVELS), F32),...  1.27 us

profile of v6, /device:TPU:1, one launch (start us, length us, event | category | flops | bytes accessed | tf_op | source)
XLA Modules:
  0.0 56.7 jit_solution(4976533842882987734)
XLA Ops:
  0.6 54.8 %scan.1.both_ref = f32[8,128]{1,0:T(8,128)} custom-call(bf16[512,2048]{1,0:T(8,128)(2,1)} %geno.1, bf16[32,512]{1,0:T(8,128)(2,1)} %bitcast.3, f32[4,512]{1,0:T(4,128)} %bitcast.4, s32[48,512]{1,0:T(8,128)} %permh.1, s32[2,64]{1,0:T(2,128)} %bitcast.5), custom_call_target="tpu_custom_call" | custom-call | tf_op jit(solution)/shard_map/scan/pallas_call | solution.py:553
  55.4 1.3 %split.1 = (f32[4,64]{1,0:T(4,128)}, f32[4,48]{1,0:T(4,128)}) custom-call(f32[8,128]{1,0:T(8,128)} %scan.1.both_ref), custom_call_target="tpu_custom_call" | custom-call | tf_op jit(solution)/shard_map/split/pallas_call | solution.py:608
